TPU v7x, 512 devices: a whole 4x4x16 slice. The times are simulated.
512 devices in a mesh: blk: 8 (over y, x_hi), grp: 64 (over z, x_lo, core).
Axes of the slice: x: 4 (x_hi: 2, x_lo: 2; x = x_hi * 2 + x_lo), y: 4, z: 16, core: 2. Of those that a mesh axis runs over, the one named last changes fastest.
Arguments:
- positions: float32 [3, 131072], P(None, ('blk', 'grp')), may hold values from -6 to 6
- velocities: float32 [3, 131072], P(None, ('blk', 'grp')), may hold values from -6 to 6
- accelerations: float32 [3, 131072], P(None, ('blk', 'grp')), may hold values from -4 to 4
- jerks: float32 [3, 131072], P(None, ('blk', 'grp')), may hold values from -4 to 4
- mass_weight: float32 [131072], P(('blk', 'grp')), may hold values from 0.3 to 3
- levels: int32 [131072], P(('blk', 'grp')), may hold values from 0 to 3, as said below
- active: int32 [2, 12288], P(None, ('blk', 'grp')), may hold values from 0 to 255, as said below
- counts: int32 [2, 512], P(None, ('blk', 'grp')), may hold values from 1 to 24
Outputs:
- positions_out: float32 [3, 131072], P(None, ('blk', 'grp'))
- velocities_out: float32 [3, 131072], P(None, ('blk', 'grp'))
- accelerations_out: float32 [3, 131072], P(None, ('blk', 'grp'))
- jerks_out: float32 [3, 131072], P(None, ('blk', 'grp'))
- fresh_forces: float32 [2, 6, 12288], P(None, None, ('blk', 'grp'))
Inputs may be any that keep to these rules, and one draw needn't show every extreme that they name: `active`: entries are local indices of the owner's particles; the live slots of one owner's list are distinct, dead slots hold 0. `levels`: particles not named in any list have level 2 or 3.
All inputs are finite; a program needn't handle non-finite values.
Results may differ from a plain program's by a relative error of at most 0.0003.
Values sent between devices are 32-bit elements; how exact they have to be, the bound alone decides.
No kernel may reach another device: no remote copies, remote signals or barrier semaphores. Data moves between devices by JAX's collectives and lax.ppermute only.
A program may use at most 64 MiB of HBM per device.

v0:
```python
import jax
import jax.numpy as jnp
from jax import lax
from jax.sharding import PartitionSpec as P

STEP_BASE = 0.125
SOFTEN = 0.01


def passed_along(value, axis, steps):
    count = lax.axis_size(axis)
    pairs = [(source, (source + steps) % count) for source in range(count)]
    return lax.ppermute(value, axis, pairs)


def predict(pos, vel, acc, jerk, elapsed):
    pred_pos = pos + elapsed * (vel + elapsed * (acc * 0.5 + elapsed * jerk / 6.0))
    pred_vel = vel + elapsed * (acc + elapsed * jerk * 0.5)
    return (pred_pos, pred_vel)


def correct(pos, vel, acc, jerk, new_acc, new_jerk, stride, hit):
    half = 0.5 * stride
    square = stride * stride / 12.0
    vel_new = vel + half * (acc + new_acc) + square * (jerk - new_jerk)
    pos_new = pos + half * (vel + vel_new) + square * (acc - new_acc)
    return (
        jnp.where(hit, pos_new, pos),
        jnp.where(hit, vel_new, vel),
        jnp.where(hit, new_acc, acc),
        jnp.where(hit, new_jerk, jerk),
    )


def block_terms(iblock, jpart):
    dpos = jpart[0:3, :, None] - iblock[0:3, None, :]
    dvel = jpart[3:6, :, None] - iblock[3:6, None, :]
    dist = dpos[0] * dpos[0] + dpos[1] * dpos[1] + dpos[2] * dpos[2] + SOFTEN
    inverse = lax.rsqrt(dist)
    weight = jpart[6][:, None] * inverse * inverse * inverse
    radial = 3.0 * (dpos[0] * dvel[0] + dpos[1] * dvel[1] + dpos[2] * dvel[2]) * inverse * inverse
    accel = jnp.sum(weight[None] * dpos, axis=1)
    jerk = jnp.sum(weight[None] * (dvel - radial[None] * dpos), axis=1)
    return jnp.concatenate([accel, jerk], axis=0)


def pair_terms(ipart, jpart):
    rows = ipart.shape[1]
    width = 512
    blocks = ipart.reshape(6, rows // width, width).transpose(1, 0, 2)
    result = lax.map(lambda iblock: block_terms(iblock, jpart), blocks)
    return result.transpose(1, 0, 2).reshape(6, rows)


def body(positions, velocities, accelerations, jerks, mass_weight, levels, active, counts):
    count_part = positions.shape[1]
    loop_len = lax.axis_size("blk")
    total_part = count_part * loop_len * lax.axis_size("grp")
    mass = mass_weight / total_part
    clock = jnp.zeros((count_part,), jnp.float32)
    stride = STEP_BASE * jnp.left_shift(jnp.ones_like(levels), levels).astype(jnp.float32)
    particle = jnp.arange(count_part, dtype=jnp.int32)
    slot = jnp.arange(active.shape[1], dtype=jnp.int32)
    pos, vel, acc, jerk = (positions, velocities, accelerations, jerks)
    recorded = []
    for step in range(2):
        now = STEP_BASE * (step + 1)
        elapsed = now - clock
        pred_pos, pred_vel = predict(pos, vel, acc, jerk, elapsed)
        live = slot < counts[step, 0]
        picker = ((active[step][:, None] == particle[None, :]) & live[:, None]).astype(jnp.float32)
        pred_both = jnp.concatenate([pred_pos, pred_vel], axis=0)
        chosen = jnp.dot(pred_both, picker.T, precision=lax.Precision.HIGHEST)
        jdata = jnp.concatenate([pred_pos, pred_vel, mass[None, :]], axis=0)
        row_actives = lax.all_gather(chosen, "grp", axis=1, tiled=True)
        travel = jdata
        partial_value = pair_terms(row_actives, travel)
        for turn in range(loop_len - 1):
            travel = passed_along(travel, "blk", 1)
            partial_value = partial_value + pair_terms(row_actives, travel)
        fresh = lax.psum_scatter(partial_value, "grp", scatter_dimension=1, tiled=True)
        recorded.append(jnp.where(live[None, :], fresh, jnp.zeros_like(fresh)))
        spread = jnp.dot(fresh, picker, precision=lax.Precision.HIGHEST)
        hit = jnp.sum(picker, axis=0) > 0.5
        pos, vel, acc, jerk = correct(pos, vel, acc, jerk, spread[0:3], spread[3:6], stride, hit)
        clock = jnp.where(hit, now, clock)
    return (pos, vel, acc, jerk, jnp.stack(recorded))


def solution(mesh):
    in_specs = (
        P(None, ("blk", "grp")),
        P(None, ("blk", "grp")),
        P(None, ("blk", "grp")),
        P(None, ("blk", "grp")),
        P(("blk", "grp")),
        P(("blk", "grp")),
        P(None, ("blk", "grp")),
        P(None, ("blk", "grp")),
    )
    out_specs = (
        P(None, ("blk", "grp")),
        P(None, ("blk", "grp")),
        P(None, ("blk", "grp")),
        P(None, ("blk", "grp")),
        P(None, None, ("blk", "grp")),
    )
    return jax.shard_map(body, mesh=mesh, in_specs=in_specs, out_specs=out_specs, check_vma=False)
```

profile of v0, /device:TPU:1, one launch (start us, length us, event | category | flops | bytes accessed | tf_op | source)
XLA Modules:
  0.0 723.3 jit_solution(7980893641859117160)
XLA Ops:
  2.1 5.5 collective-permute-start
  7.6 1.3 fusion.138
  10.6 70.2 %all-gather = f32[64,24,6]{1,2,0:T(8,128)S(1)} all-gather(f32[1,24,6]{1,2,0:T(8,128)S(1)} %convolution_bitcast_fusion.1), channel_id=1, replica_groups=mesh['blk'=8,'grp'=64] {'grp'}, dimensions={0}, use_global_device_ids=true | all-gather | bytes 37440 | tf_op jit(solution)/shard_map/all_gather | solution.py:75
  81.1 3.7 while.160
  86.2 1.3 dynamic-slice
  88.1 4.7 collective-permute-start.1
  92.8 8.1 %while.161 = (s32[]{:T(128)}, f32[3,6,512]{2,1,0:T(8,128)S(1)}, f32[7,256]{1,0:T(8,128)}, f32[3,6,512]{2,1,0:T(8,128)S(1)}, s32[]{:T(128)}, /*index=5*/s32[]{:T(128)}, s32[]{}) while((s32[]{:T(128)}, f32[3,6,512]{2,1,0:T(8,128)S(1)}, f32[7,256]{1,0:T(8,128)}, f32[3,6,512]{2,1,0:T(8,128)S(1)}, s32[]{:T(128)}, /*index=5*/s32[]{:T(128)}, ...), condition=%wide.region_9.10_spmd, body=%wide.region_6.9_spmd.sunk | while | flops 6160387 | bytes 8510565 | solution.py:51
  95.5 0.8 fusion.187
  98.2 0.8 fusion.187
  100.9 3.1 collective-permute-start.2
  104.0 8.1 %while.162 = (s32[]{:T(128)}, f32[3,6,512]{2,1,0:T(8,128)S(1)}, f32[7,256]{1,0:T(8,128)}, f32[3,6,512]{2,1,0:T(8,128)S(1)}, s32[]{:T(128)}, /*index=5*/s32[]{:T(128)}, s32[]{}) while((s32[]{:T(128)}, f32[3,6,512]{2,1,0:T(8,128)S(1)}, f32[7,256]{1,0:T(8,128)}, f32[3,6,512]{2,1,0:T(8,128)S(1)}, s32[]{:T(128)}, /*index=5*/s32[]{:T(128)}, ...), condition=%wide.region_13.14_spmd, body=%wide.region_10.13_spmd.sunk | while | flops 6160387 | bytes 8510565 | solution.py:51
  104.1 0.8 fusion.190
  106.8 0.8 fusion.190
  109.5 0.8 fusion.190
  112.1 4.7 collective-permute-start.3
  116.9 8.1 %while.163 = (s32[]{:T(128)}, f32[3,6,512]{2,1,0:T(8,128)S(1)}, f32[7,256]{1,0:T(8,128)}, f32[3,6,512]{2,1,0:T(8,128)S(1)}, s32[]{:T(128)}, /*index=5*/s32[]{:T(128)}, s32[]{}) while((s32[]{:T(128)}, f32[3,6,512]{2,1,0:T(8,128)S(1)}, f32[7,256]{1,0:T(8,128)}, f32[3,6,512]{2,1,0:T(8,128)S(1)}, s32[]{:T(128)}, /*index=5*/s32[]{:T(128)}, ...), condition=%wide.region_17.18_spmd, body=%wide.region_14.17_spmd.sunk | while | flops 6160387 | bytes 8510565 | solution.py:51
  116.9 0.8 fusion.193
  119.6 0.8 fusion.193
  122.3 0.8 fusion.193
  125.0 3.1 collective-permute-start.4
  128.1 8.1 %while.164 = (s32[]{:T(128)}, f32[3,6,512]{2,1,0:T(8,128)S(1)}, f32[7,256]{1,0:T(8,128)}, f32[3,6,512]{2,1,0:T(8,128)S(1)}, s32[]{:T(128)}, /*index=5*/s32[]{:T(128)}, s32[]{}) while((s32[]{:T(128)}, f32[3,6,512]{2,1,0:T(8,128)S(1)}, f32[7,256]{1,0:T(8,128)}, f32[3,6,512]{2,1,0:T(8,128)S(1)}, s32[]{:T(128)}, /*index=5*/s32[]{:T(128)}, ...), condition=%wide.region_21.22_spmd, body=%wide.region_18.21_spmd.sunk | while | flops 6160387 | bytes 8510565 | solution.py:51
  128.2 0.8 fusion.196
  130.9 0.8 fusion.196
  133.6 0.8 fusion.196
  136.2 4.4 collective-permute-start.5
  140.7 8.1 %while.165 = (s32[]{:T(128)}, f32[3,6,512]{2,1,0:T(8,128)S(1)}, f32[7,256]{1,0:T(8,128)}, f32[3,6,512]{2,1,0:T(8,128)S(1)}, s32[]{:T(128)}, /*index=5*/s32[]{:T(128)}, s32[]{}) while((s32[]{:T(128)}, f32[3,6,512]{2,1,0:T(8,128)S(1)}, f32[7,256]{1,0:T(8,128)}, f32[3,6,512]{2,1,0:T(8,128)S(1)}, s32[]{:T(128)}, /*index=5*/s32[]{:T(128)}, ...), condition=%wide.region_25.26_spmd, body=%wide.region_22.25_spmd.sunk | while | flops 6160387 | bytes 8510565 | solution.py:51
  140.7 0.8 fusion.199
  143.4 0.8 fusion.199
  146.1 0.8 fusion.199
  148.8 3.1 collective-permute-start.6
  151.9 8.1 %while.166 = (s32[]{:T(128)}, f32[3,6,512]{2,1,0:T(8,128)S(1)}, f32[7,256]{1,0:T(8,128)}, f32[3,6,512]{2,1,0:T(8,128)S(1)}, s32[]{:T(128)}, /*index=5*/s32[]{:T(128)}, s32[]{}) while((s32[]{:T(128)}, f32[3,6,512]{2,1,0:T(8,128)S(1)}, f32[7,256]{1,0:T(8,128)}, f32[3,6,512]{2,1,0:T(8,128)S(1)}, s32[]{:T(128)}, /*index=5*/s32[]{:T(128)}, ...), condition=%wide.region_29.30_spmd, body=%wide.region_26.29_spmd.sunk | while | flops 6160387 | bytes 8510565 | solution.py:51
  154.6 0.8 fusion.202
  157.3 0.8 fusion.202
  160.1 3.7 while.167
  163.8 204.8 %all-reduce = f32[6,1536]{1,0:T(8,128)S(1)} all-reduce(f32[6,1536]{1,0:T(8,128)S(1)} %bitcast.364), channel_id=2, replica_groups=mesh['blk'=8,'grp'=64] {'grp'}, use_global_device_ids=true, to_apply=%region_34.35.clone | all-reduce | flops 9216 | bytes 73728
  369.1 64.4 %all-gather.1 = f32[64,24,6]{1,2,0:T(8,128)S(1)} all-gather(f32[1,24,6]{1,2,0:T(8,128)S(1)} %convolution_bitcast_fusion), channel_id=1, replica_groups=mesh['blk'=8,'grp'=64] {'grp'}, dimensions={0}, use_global_device_ids=true | all-gather | bytes 37440 | tf_op jit(solution)/shard_map/all_gather | solution.py:75
  433.8 3.3 collective-permute-start.7
  437.2 3.7 while.168
  440.9 1.0 collective-permute-done.7
  441.9 2.1 collective-permute-start.8
  444.1 8.1 %while.169 = (s32[]{:T(128)}, f32[3,6,512]{2,1,0:T(8,128)S(1)}, f32[7,256]{1,0:T(8,128)}, f32[3,6,512]{2,1,0:T(8,128)S(1)}, s32[]{:T(128)}, /*index=5*/s32[]{:T(128)}, s32[]{}) while((s32[]{:T(128)}, f32[3,6,512]{2,1,0:T(8,128)S(1)}, f32[7,256]{1,0:T(8,128)}, f32[3,6,512]{2,1,0:T(8,128)S(1)}, s32[]{:T(128)}, /*index=5*/s32[]{:T(128)}, ...), condition=%wide.region_42.43_spmd, body=%wide.region_39.42_spmd.sunk | while | flops 6160387 | bytes 8510565 | solution.py:51
  444.1 0.8 fusion.210
  446.8 0.8 fusion.210
  449.5 0.8 fusion.210
  452.2 4.7 collective-permute-start.9
  456.9 8.1 %while.170 = (s32[]{:T(128)}, f32[3,6,512]{2,1,0:T(8,128)S(1)}, f32[7,256]{1,0:T(8,128)}, f32[3,6,512]{2,1,0:T(8,128)S(1)}, s32[]{:T(128)}, /*index=5*/s32[]{:T(128)}, s32[]{}) while((s32[]{:T(128)}, f32[3,6,512]{2,1,0:T(8,128)S(1)}, f32[7,256]{1,0:T(8,128)}, f32[3,6,512]{2,1,0:T(8,128)S(1)}, s32[]{:T(128)}, /*index=5*/s32[]{:T(128)}, ...), condition=%wide.region_46.47_spmd, body=%wide.region_43.46_spmd.sunk | while | flops 6160387 | bytes 8510565 | solution.py:51
  456.9 0.8 fusion.213
  459.6 0.8 fusion.213
  462.3 0.8 fusion.213
  465.0 3.1 collective-permute-start.10
  468.2 8.1 %while.171 = (s32[]{:T(128)}, f32[3,6,512]{2,1,0:T(8,128)S(1)}, f32[7,256]{1,0:T(8,128)}, f32[3,6,512]{2,1,0:T(8,128)S(1)}, s32[]{:T(128)}, /*index=5*/s32[]{:T(128)}, s32[]{}) while((s32[]{:T(128)}, f32[3,6,512]{2,1,0:T(8,128)S(1)}, f32[7,256]{1,0:T(8,128)}, f32[3,6,512]{2,1,0:T(8,128)S(1)}, s32[]{:T(128)}, /*index=5*/s32[]{:T(128)}, ...), condition=%wide.region_50.51_spmd, body=%wide.region_47.50_spmd.sunk | while | flops 6160387 | bytes 8510565 | solution.py:51
  468.2 0.8 fusion.216
  470.9 0.8 fusion.216
  473.6 0.8 fusion.216
  476.3 4.7 collective-permute-start.11
  481.0 8.1 %while.172 = (s32[]{:T(128)}, f32[3,6,512]{2,1,0:T(8,128)S(1)}, f32[7,256]{1,0:T(8,128)}, f32[3,6,512]{2,1,0:T(8,128)S(1)}, s32[]{:T(128)}, /*index=5*/s32[]{:T(128)}, s32[]{}) while((s32[]{:T(128)}, f32[3,6,512]{2,1,0:T(8,128)S(1)}, f32[7,256]{1,0:T(8,128)}, f32[3,6,512]{2,1,0:T(8,128)S(1)}, s32[]{:T(128)}, /*index=5*/s32[]{:T(128)}, ...), condition=%wide.region_54.55_spmd, body=%wide.region_51.54_spmd.sunk | while | flops 6160387 | bytes 8510565 | solution.py:51
  481.0 0.8 fusion.219
  483.7 0.8 fusion.219
  489.1 3.1 collective-permute-start.12
  492.3 8.1 %while.173 = (s32[]{:T(128)}, f32[3,6,512]{2,1,0:T(8,128)S(1)}, f32[7,256]{1,0:T(8,128)}, f32[3,6,512]{2,1,0:T(8,128)S(1)}, s32[]{:T(128)}, /*index=5*/s32[]{:T(128)}, s32[]{}) while((s32[]{:T(128)}, f32[3,6,512]{2,1,0:T(8,128)S(1)}, f32[7,256]{1,0:T(8,128)}, f32[3,6,512]{2,1,0:T(8,128)S(1)}, s32[]{:T(128)}, /*index=5*/s32[]{:T(128)}, ...), condition=%wide.region_58.59_spmd, body=%wide.region_55.58_spmd.sunk | while | flops 6160387 | bytes 8510565 | solution.py:51
  500.4 4.4 collective-permute-start.13
  504.8 8.1 %while.174 = (s32[]{:T(128)}, f32[3,6,512]{2,1,0:T(8,128)S(1)}, f32[7,256]{1,0:T(8,128)}, f32[3,6,512]{2,1,0:T(8,128)S(1)}, s32[]{:T(128)}, /*index=5*/s32[]{:T(128)}, s32[]{}) while((s32[]{:T(128)}, f32[3,6,512]{2,1,0:T(8,128)S(1)}, f32[7,256]{1,0:T(8,128)}, f32[3,6,512]{2,1,0:T(8,128)S(1)}, s32[]{:T(128)}, /*index=5*/s32[]{:T(128)}, ...), condition=%wide.region_62.63_spmd, body=%wide.region_59.62_spmd.sunk | while | flops 6160387 | bytes 8510565 | solution.py:51
  512.9 3.7 while.175
  516.7 205.1 %all-reduce.1 = f32[6,1536]{1,0:T(8,128)S(1)} all-reduce(f32[6,1536]{1,0:T(8,128)S(1)} %bitcast.365), channel_id=3, replica_groups=mesh['blk'=8,'grp'=64] {'grp'}, use_global_device_ids=true, to_apply=%region_67.68.clone | all-reduce | flops 9216 | bytes 73728
  (371 shorter events, 96.1 us)
Async XLA Ops:
  2.1 86.0 %collective-permute-start = (f32[7,256]{1,0:T(8,128)S(1)}, f32[7,256]{1,0:T(8,128)}, u32[]{:S(2)}, u32[]{:S(2)}) collective-permute-start(f32[7,256]{1,0:T(8,128)S(1)} %pad_maximum_fusion.1), channel_id=1, source_target_pairs={{0,64},{64,128},{128,192},{192,256},{256,320},{320,384},{384,448},... | collective-permute-start | bytes 21512 | tf_op jit(solution)/shard_map/ppermute | solution.py:13
  81.1 3.7 copy-start.4
  88.1 12.8 %collective-permute-start.1 = (f32[7,256]{1,0:T(8,128)}, f32[7,256]{1,0:T(8,128)}, u32[]{:S(2)}, u32[]{:S(2)}) collective-permute-start(f32[7,256]{1,0:T(8,128)} %collective-permute-done), channel_id=1, source_target_pairs={{0,64},{64,128},{128,192},{192,256},{256,320},{320,384},{384,448},... | collective-permute-start | bytes 21512 | tf_op jit(solution)/shard_map/ppermute | solution.py:13
  100.9 11.3 %collective-permute-start.2 = (f32[7,256]{1,0:T(8,128)}, f32[7,256]{1,0:T(8,128)}, u32[]{:S(2)}, u32[]{:S(2)}) collective-permute-start(f32[7,256]{1,0:T(8,128)} %collective-permute-done.1), channel_id=1, source_target_pairs={{0,64},{64,128},{128,192},{192,256},{256,320},{320,384},{384,448},... | collective-permute-start | bytes 21512 | tf_op jit(solution)/shard_map/ppermute | solution.py:13
  112.1 12.8 %collective-permute-start.3 = (f32[7,256]{1,0:T(8,128)}, f32[7,256]{1,0:T(8,128)}, u32[]{:S(2)}, u32[]{:S(2)}) collective-permute-start(f32[7,256]{1,0:T(8,128)} %collective-permute-done.2), channel_id=1, source_target_pairs={{0,64},{64,128},{128,192},{192,256},{256,320},{320,384},{384,448},... | collective-permute-start | bytes 21512 | tf_op jit(solution)/shard_map/ppermute | solution.py:13
  125.0 11.3 %collective-permute-start.4 = (f32[7,256]{1,0:T(8,128)}, f32[7,256]{1,0:T(8,128)}, u32[]{:S(2)}, u32[]{:S(2)}) collective-permute-start(f32[7,256]{1,0:T(8,128)} %collective-permute-done.3), channel_id=1, source_target_pairs={{0,64},{64,128},{128,192},{192,256},{256,320},{320,384},{384,448},... | collective-permute-start | bytes 21512 | tf_op jit(solution)/shard_map/ppermute | solution.py:13
  136.2 12.5 %collective-permute-start.5 = (f32[7,256]{1,0:T(8,128)}, f32[7,256]{1,0:T(8,128)}, u32[]{:S(2)}, u32[]{:S(2)}) collective-permute-start(f32[7,256]{1,0:T(8,128)} %collective-permute-done.4), channel_id=1, source_target_pairs={{0,64},{64,128},{128,192},{192,256},{256,320},{320,384},{384,448},... | collective-permute-start | bytes 21512 | tf_op jit(solution)/shard_map/ppermute | solution.py:13
  148.8 11.2 %collective-permute-start.6 = (f32[7,256]{1,0:T(8,128)}, f32[7,256]{1,0:T(8,128)S(1)}, u32[]{:S(2)}, u32[]{:S(2)}) collective-permute-start(f32[7,256]{1,0:T(8,128)} %collective-permute-done.5), channel_id=1, source_target_pairs={{0,64},{64,128},{128,192},{192,256},{256,320},{320,384},{384,448},... | collective-permute-start | bytes 21512 | tf_op jit(solution)/shard_map/ppermute | solution.py:13
  160.0 208.8 %copy-start = (f32[3,256]{1,0:T(4,128)S(1)}, f32[3,256]{1,0:T(4,128)}, u32[]{:S(2)}) copy-start(f32[3,256]{1,0:T(4,128)} %param.43) | copy-start | bytes 9220
  160.0 208.8 %copy-start.1 = (f32[3,256]{1,0:T(4,128)S(1)}, f32[3,256]{1,0:T(4,128)}, u32[]{:S(2)}) copy-start(f32[3,256]{1,0:T(4,128)} %param.40) | copy-start | bytes 9220
  160.0 208.8 %copy-start.2 = (f32[3,256]{1,0:T(4,128)S(1)}, f32[3,256]{1,0:T(4,128)}, u32[]{:S(2)}) copy-start(f32[3,256]{1,0:T(4,128)} %param.41) | copy-start | bytes 9220
  160.0 208.8 %copy-start.3 = (f32[3,256]{1,0:T(4,128)S(1)}, f32[3,256]{1,0:T(4,128)}, u32[]{:S(2)}) copy-start(f32[3,256]{1,0:T(4,128)} %param.42) | copy-start | bytes 9220
  433.8 8.1 %collective-permute-start.7 = (f32[7,256]{1,0:T(8,128)S(1)}, f32[7,256]{1,0:T(8,128)}, u32[]{:S(2)}, u32[]{:S(2)}) collective-permute-start(f32[7,256]{1,0:T(8,128)S(1)} %pad_maximum_fusion), channel_id=1, source_target_pairs={{0,64},{64,128},{128,192},{192,256},{256,320},{320,384},{384,448},... | collective-permute-start | bytes 21512 | tf_op jit(solution)/shard_map/ppermute | solution.py:13
  441.9 10.2 %collective-permute-start.8 = (f32[7,256]{1,0:T(8,128)}, f32[7,256]{1,0:T(8,128)}, u32[]{:S(2)}, u32[]{:S(2)}) collective-permute-start(f32[7,256]{1,0:T(8,128)} %collective-permute-done.7), channel_id=1, source_target_pairs={{0,64},{64,128},{128,192},{192,256},{256,320},{320,384},{384,448},... | collective-permute-start | bytes 21512 | tf_op jit(solution)/shard_map/ppermute | solution.py:13
  452.2 12.8 %collective-permute-start.9 = (f32[7,256]{1,0:T(8,128)}, f32[7,256]{1,0:T(8,128)}, u32[]{:S(2)}, u32[]{:S(2)}) collective-permute-start(f32[7,256]{1,0:T(8,128)} %collective-permute-done.8), channel_id=1, source_target_pairs={{0,64},{64,128},{128,192},{192,256},{256,320},{320,384},{384,448},... | collective-permute-start | bytes 21512 | tf_op jit(solution)/shard_map/ppermute | solution.py:13
  465.0 11.3 %collective-permute-start.10 = (f32[7,256]{1,0:T(8,128)}, f32[7,256]{1,0:T(8,128)}, u32[]{:S(2)}, u32[]{:S(2)}) collective-permute-start(f32[7,256]{1,0:T(8,128)} %collective-permute-done.9), channel_id=1, source_target_pairs={{0,64},{64,128},{128,192},{192,256},{256,320},{320,384},{384,448},... | collective-permute-start | bytes 21512 | tf_op jit(solution)/shard_map/ppermute | solution.py:13
  476.3 12.8 %collective-permute-start.11 = (f32[7,256]{1,0:T(8,128)}, f32[7,256]{1,0:T(8,128)}, u32[]{:S(2)}, u32[]{:S(2)}) collective-permute-start(f32[7,256]{1,0:T(8,128)} %collective-permute-done.10), channel_id=1, source_target_pairs={{0,64},{64,128},{128,192},{192,256},{256,320},{320,384},{384,448},... | collective-permute-start | bytes 21512 | tf_op jit(solution)/shard_map/ppermute | solution.py:13
  489.1 11.3 %collective-permute-start.12 = (f32[7,256]{1,0:T(8,128)}, f32[7,256]{1,0:T(8,128)}, u32[]{:S(2)}, u32[]{:S(2)}) collective-permute-start(f32[7,256]{1,0:T(8,128)} %collective-permute-done.11), channel_id=1, source_target_pairs={{0,64},{64,128},{128,192},{192,256},{256,320},{320,384},{384,448},... | collective-permute-start | bytes 21512 | tf_op jit(solution)/shard_map/ppermute | solution.py:13
  500.4 12.5 %collective-permute-start.13 = (f32[7,256]{1,0:T(8,128)}, f32[7,256]{1,0:T(8,128)S(1)}, u32[]{:S(2)}, u32[]{:S(2)}) collective-permute-start(f32[7,256]{1,0:T(8,128)} %collective-permute-done.12), channel_id=1, source_target_pairs={{0,64},{64,128},{128,192},{192,256},{256,320},{320,384},{384,448},... | collective-permute-start | bytes 21512 | tf_op jit(solution)/shard_map/ppermute | solution.py:13
  512.9 209.8 %copy-start.5 = (pred[256]{0:T(512)(128)(4,1)S(1)}, pred[256]{0:T(512)(128)(4,1)}, u32[]{:S(2)}) copy-start(pred[256]{0:T(512)(128)(4,1)} %broadcast_compare_fusion.1) | copy-start | bytes 772
where the time goes:
time: 733 us; the launch traced here: 723 us
  blocking collectives  545 us (74%)
  other arithmetic  60.6 us (8%)
  local copies, waits for them, and re-layouts  58.3 us (8%)
  starting transfers between devices  54 us (7%)
    unnamed x2, blocking collectives  410 us
    all_gather x2, blocking collectives, body(): row_actives = lax.all_gather(chosen, 'grp', axis=1, tiled=True)  135 us
    ppermute x14, starting transfers between devices, passed_along(): return lax.ppermute(value, axis, pairs)  54 us
    slice x42, local copies, waits for them, and re-layouts, block_terms(): dvel = jpart[3:6, :, None] - iblock[3:6, None, :]  27.9 us
    reduce_sum x48, other arithmetic, block_terms(): accel = jnp.sum(weight[None] * dpos, axis=1)  27.4 us
    slice x42, local copies, waits for them, and re-layouts, block_terms(): weight = jpart[6][:, None] * inverse * inverse * inverse  25.3 us
    mul x48, other arithmetic, block_terms(): jerk = jnp.sum(weight[None] * (dvel - radial[None] * dpos), axis=1)  15.3 us
  transfers between devices with their start and end apart: 14, of which 1 were waited for; matrix products, arithmetic and copies ran while one was open for 15% of the time, Pallas kernels for 0%

commit v1 on v0

v1 whole, which is shorter than its diff:
```python
import jax
import jax.numpy as jnp
from jax import lax
from jax.experimental import pallas as pl
from jax.experimental.pallas import tpu as pltpu
from jax.sharding import Mesh, PartitionSpec as P

STEP_BASE = 0.125
SOFTEN = 0.01
PART = 256
SLOTS = 24
CHIPS = 16
PLANE = 2 * CHIPS
COLUMN = 16
COLS = SLOTS * CHIPS
SHARE = SLOTS // 2
LANES = 128
LISTED = 32
RATES = 64
ALL_AXES = ("y", "h", "z", "l", "c")
PLANE_AXES = ("y", "h", "l", "c")
EXACT = lax.Precision.HIGHEST
F32 = jnp.float32
I32 = jnp.int32
NT = (((1,), (1,)), ((), ()))


def predict(pos, vel, acc, jerk, elapsed):
    pred_pos = pos + elapsed * (vel + elapsed * (acc * 0.5 + elapsed * jerk / 6.0))
    pred_vel = vel + elapsed * (acc + elapsed * jerk * 0.5)
    return (pred_pos, pred_vel)


def correct(pos, vel, acc, jerk, new_acc, new_jerk, stride):
    half = 0.5 * stride
    square = stride * stride / 12.0
    vel_new = vel + half * (acc + new_acc) + square * (jerk - new_jerk)
    pos_new = pos + half * (vel + vel_new) + square * (acc - new_acc)
    return (pos_new, vel_new)


def iota(shape, axis):
    return lax.broadcasted_iota(I32, shape, axis)


def prepare_kernel(total, cnt, pos, vel, acc, jerk, weight, levels, active, zsend, isend, place, slots, jrows, srows):
    core = lax.axis_index("c")
    mass = weight[...] / total
    lev = levels[...]
    p, v, a, j = pos[...], vel[...], acc[...], jerk[...]
    p1, v1 = predict(p, v, a, j, STEP_BASE)
    p2, v2 = predict(p, v, a, j, 2 * STEP_BASE)
    jrows[0:3] = p1
    jrows[3:6] = v1
    jrows[6:7] = mass
    jrows[7:8] = jnp.where(lev == 0, 0.0, mass)
    jrows[8:11] = p2
    jrows[11:14] = v2
    jrows[14:16] = jnp.zeros((2, PART), F32)
    rows = jrows[...]
    for k in range(COLUMN):
        zsend[k] = rows
    srows[...] = jnp.zeros(srows.shape, F32)
    srows[0:3] = p
    srows[3:6] = v
    srows[6:7] = mass
    srows[8:11] = p2
    srows[11:14] = v2
    srows[16:19] = a
    srows[19:22] = j

    n1, n2 = cnt[0, 0], cnt[1, 0]
    off0 = jnp.where(core == 1, SLOTS - n1, 0)
    off1 = jnp.where(core == 1, n1, 0)
    who = iota((PART, SLOTS), 0)
    slot = iota((PART, SLOTS), 1)
    a1 = ((who == active[0:1, :]) & (slot < n1)).astype(F32)
    a2 = ((who == active[1:2, :]) & (slot < n2)).astype(F32)
    col = iota((LANES, SLOTS), 0)
    cslot = iota((LANES, SLOTS), 1)
    first = (col == cslot + off0) & (cslot < n1)
    again = (col == cslot + off0 + RATES) & (cslot < n1)
    first_f = first.astype(F32)
    listed = jnp.dot(jnp.broadcast_to(lev.astype(F32), (8, PART)), a2, preferred_element_type=F32)
    live = iota((8, SLOTS), 1) < n2
    is0 = (live & (listed < 0.5)).astype(F32)
    is1 = (live & (listed > 0.5) & (listed < 1.5)).astype(F32)
    before = (iota((SLOTS, SLOTS), 0) < iota((SLOTS, SLOTS), 1)).astype(F32)
    rank0 = jnp.dot(is0, before, preferred_element_type=F32)[0:1].astype(I32)
    rank1 = jnp.dot(is1, before, preferred_element_type=F32)[0:1].astype(I32)
    second = ((col == rank1 + (off1 + LISTED)) & (is1[0:1] > 0.5)).astype(F32)
    held = ((col == rank0 + off0) & (is0[0:1] > 0.5)).astype(F32)
    spots = lax.dot_general(a1, first_f + again.astype(F32), NT, preferred_element_type=F32)
    spots = spots + lax.dot_general(a2, second, NT, preferred_element_type=F32)
    place[...] = spots
    slots[0] = first_f
    slots[1] = held + second
    picked = jnp.dot(srows[...], spots, precision=EXACT, preferred_element_type=F32)
    lane = iota((8, LANES), 1)
    payload = jnp.where(lane < LISTED, picked[0:8], jnp.where(lane < RATES, picked[8:16], picked[16:24]))
    for k in range(PLANE):
        isend[k] = payload


def gather_terms(jt, bases, rows, targets, sums):
    def one(t, sums):
        sums = list(sums)
        tile = jt[pl.ds(pl.multiple_of(t * 8, 8), 8), :]
        for base in bases:
            cols = [jnp.broadcast_to(tile[:, k : k + 1], (8, LANES)) for k in base]
            for i, target in enumerate(targets):
                dx, dy, dz = (cols[k] - target[k] for k in range(3))
                du, dv, dw = (cols[k] - target[k] for k in range(3, 6))
                inv = lax.rsqrt(dx * dx + dy * dy + dz * dz + SOFTEN)
                inv2 = inv * inv
                weight = cols[6] * inv * inv2
                radial = (dx * du + dy * dv + dz * dw) * (inv2 * 3.0)
                ax, ay, az, jx, jy, jz = sums[6 * i : 6 * i + 6]
                sums[6 * i : 6 * i + 6] = (
                    ax + weight * dx,
                    ay + weight * dy,
                    az + weight * dz,
                    jx + weight * (du - radial * dx),
                    jy + weight * (dv - radial * dy),
                    jz + weight * (dw - radial * dz),
                )
        return tuple(sums)

    return lax.fori_loop(0, rows // 8, one, sums)


def tiles_of(states):
    return [
        [jnp.broadcast_to(states[k : k + 1, LANES * t : LANES * (t + 1)], (8, LANES)) for k in range(6)]
        for t in range(states.shape[1] // LANES)
    ]


def zero_sums(count):
    return tuple(jnp.zeros((8, LANES), F32) for _ in range(6 * count))


def store_sums(out, sums):
    out[6:8] = jnp.zeros((2, out.shape[1]), F32)
    for i in range(len(sums) // 6):
        for k in range(6):
            out[k : k + 1, LANES * i : LANES * (i + 1)] = jnp.sum(sums[6 * i + k], axis=0, keepdims=True)


def first_bases():
    return [[16 * s + k for k in range(7)] for s in range(COLUMN)]


def later_bases():
    return [[16 * s + k for k in (8, 9, 10, 11, 12, 13, 7)] for s in range(COLUMN)]


def first_kernel(zrecv, irecv, psend, known, other, jt, part):
    jt[...] = jnp.transpose(zrecv[...].reshape(COLUMN * 16, PART))
    for q in range(CHIPS):
        block = irecv[2 * q] + irecv[2 * q + 1]
        here = slice(SLOTS * q, SLOTS * (q + 1))
        known[0:8, here] = block[:, 0:SLOTS]
        known[8:16, here] = block[:, RATES : RATES + SLOTS]
        other[:, here] = block[:, LISTED : LISTED + SLOTS]
    p1, v1 = predict(known[0:3], known[3:6], known[8:11], known[11:14], STEP_BASE)
    states = jnp.concatenate([p1, v1], axis=0)
    targets = tiles_of(states)
    sums = gather_terms(jt, first_bases(), PART, targets, zero_sums(len(targets)))
    store_sums(part, sums)
    whole = part[...]
    for k in range(PLANE):
        psend[k] = whole


def later_kernel(jt, states, out):
    targets = tiles_of(states[...])
    sums = gather_terms(jt, later_bases(), PART, targets, zero_sums(len(targets)))
    store_sums(out, sums)


def update_kernel(precv, known, zsend, moved, mine):
    total = precv[0]
    for k in range(1, PLANE):
        total = total + precv[k]
    p, v, a, j = known[0:3], known[3:6], known[8:11], known[11:14]
    new_a, new_j = total[0:3], total[3:6]
    pos, vel = correct(p, v, a, j, new_a, new_j, STEP_BASE)
    p2, v2 = predict(pos, vel, new_a, new_j, STEP_BASE)
    moved[0:3] = p2
    moved[3:6] = v2
    moved[6:7] = known[6:7]
    moved[7:8] = jnp.zeros((1, COLS), F32)
    chip = (lax.axis_index("y") * 2 + lax.axis_index("h")) * 2 + lax.axis_index("l")
    core = lax.axis_index("c")
    row = iota((COLS, LANES), 0)
    lane = iota((COLS, LANES), 1)
    share = ((row == lane + (chip * SLOTS + core * SHARE)) & (lane < SHARE)).astype(F32)
    block = ((row == lane + chip * SLOTS) & (lane < SLOTS)).astype(F32)
    payload = jnp.dot(moved[...], share, precision=EXACT, preferred_element_type=F32)
    for k in range(COLUMN):
        zsend[k] = payload
    mine[...] = jnp.dot(total, block, precision=EXACT, preferred_element_type=F32)


def last_kernel(zrecv, moved, other, part0, part1, fsend, jt, sum0, sum1):
    jt[...] = jnp.transpose(zrecv[...].reshape(COLUMN * 8, LANES))
    bases = [[8 * s + k for k in range(7)] for s in range(COLUMN)]
    for states, part, out in ((moved, part0, sum0), (other, part1, sum1)):
        targets = tiles_of(states[...])
        sums = gather_terms(jt, bases, 16, targets, zero_sums(len(targets)))
        store_sums(out, sums)
        out[...] = out[...] + part[...]
    for q in range(CHIPS):
        here = slice(SLOTS * q, SLOTS * (q + 1))
        for k in (2 * q, 2 * q + 1):
            fsend[k] = jnp.zeros((8, LANES), F32)
            fsend[k, :, 0:SLOTS] = sum0[:, here]
            fsend[k, :, LISTED : LISTED + SLOTS] = sum1[:, here]


def finish_kernel(pos, vel, acc, jerk, levels, frecv, mine, place, slots, pos_o, vel_o, acc_o, jerk_o, fresh):
    total = frecv[0]
    for k in range(1, PLANE):
        total = total + frecv[k]
    once = mine[...]
    fresh[0] = jnp.dot(once, slots[0], precision=EXACT, preferred_element_type=F32)[0:6]
    fresh[1] = jnp.dot(total, slots[1], precision=EXACT, preferred_element_type=F32)[0:6]
    lane = iota((8, LANES), 1)
    spots = place[...]
    lev = levels[...]
    stride = STEP_BASE * jnp.left_shift(jnp.ones_like(lev), lev).astype(F32)
    p, v, a, j = pos[...], vel[...], acc[...], jerk[...]
    for step, values in enumerate((once, total)):
        spread = lax.dot_general(jnp.where(lane < RATES, values, 0.0), spots, NT, precision=EXACT, preferred_element_type=F32)
        new_a, new_j = spread[0:3], spread[3:6]
        hit = lev <= step
        p_new, v_new = correct(p, v, a, j, new_a, new_j, stride)
        p, v = jnp.where(hit, p_new, p), jnp.where(hit, v_new, v)
        a, j = jnp.where(hit, new_a, a), jnp.where(hit, new_j, j)
    pos_o[...] = p
    vel_o[...] = v
    acc_o[...] = a
    jerk_o[...] = j


def call(kernel, ins, outs, scratch=(), smem=0, pairs=0):
    vmem = pl.BlockSpec(memory_space=pltpu.VMEM)
    ops = max(pairs * 40, 1000)
    return pl.pallas_call(
        kernel,
        out_shape=[jax.ShapeDtypeStruct(s, F32) for s in outs],
        in_specs=[pl.BlockSpec(memory_space=pltpu.SMEM)] * smem + [vmem] * (len(ins) - smem),
        out_specs=[vmem] * len(outs),
        scratch_shapes=[pltpu.VMEM(s, F32) for s in scratch],
        compiler_params=pltpu.CompilerParams(vmem_limit_bytes=32 * 1024 * 1024),
        cost_estimate=pl.CostEstimate(flops=ops, bytes_accessed=65536, transcendentals=pairs),
    )(*ins)


def exchange(value, axes):
    return lax.all_to_all(value, axes, 0, 0, tiled=True)


def body(positions, velocities, accelerations, jerks, mass_weight, levels, active, counts):
    total_part = PART * lax.axis_size(ALL_AXES)
    lev = levels.reshape(1, PART)
    state = (positions, velocities, accelerations, jerks)

    def prepare(*refs):
        prepare_kernel(total_part, *refs)

    zsend, isend, place, slots = call(
        prepare,
        (counts, *state, mass_weight.reshape(1, PART), lev, active),
        [(COLUMN, 16, PART), (PLANE, 8, LANES), (PART, LANES), (2, LANES, SLOTS)],
        [(16, PART), (24, PART)],
        smem=1,
    )
    irecv = exchange(isend, PLANE_AXES)
    zrecv = exchange(zsend, "z")
    pairs = COLS * PART * COLUMN
    psend, known, other, jt = call(
        first_kernel,
        (zrecv, irecv),
        [(PLANE, 8, COLS), (16, COLS), (8, COLS), (PART, PART)],
        [(8, COLS)],
        pairs=pairs,
    )
    precv = exchange(psend, PLANE_AXES)
    (part1,) = call(later_kernel, (jt, other), [(8, COLS)], pairs=pairs)
    zsend2, moved, mine = call(update_kernel, (precv, known), [(COLUMN, 8, LANES), (8, COLS), (8, LANES)])
    zrecv2 = exchange(zsend2, "z")
    (part0,) = call(later_kernel, (jt, moved), [(8, COLS)], pairs=pairs)
    (fsend,) = call(
        last_kernel,
        (zrecv2, moved, other, part0, part1),
        [(PLANE, 8, LANES)],
        [(LANES, LANES), (8, COLS), (8, COLS)],
    )
    frecv = exchange(fsend, PLANE_AXES)
    return call(
        finish_kernel,
        (*state, lev, frecv, mine, place, slots),
        [(3, PART)] * 4 + [(2, 6, SLOTS)],
    )


def solution(mesh):
    fine = Mesh(mesh.devices.reshape(4, 2, 16, 2, 2), ALL_AXES)
    rows, flat = P(None, ALL_AXES), P(ALL_AXES)
    in_specs = (rows, rows, rows, rows, flat, flat, rows, rows)
    out_specs = (rows, rows, rows, rows, P(None, None, ALL_AXES))
    return jax.shard_map(body, mesh=fine, in_specs=in_specs, out_specs=out_specs, check_vma=False)
```

time: 733 us -> 128 us (0.17); the launches traced: 723 us -> 128 us
  blocking collectives: 545 us -> 74.7 us
  other arithmetic: 60.6 us -> 0 us
  local copies, waits for them, and re-layouts: 58.3 us -> 6.13 us
  starting transfers between devices: 54 us -> 5.66 us
  Pallas kernels: 0 us -> 40.5 us
    unnamed x2 -> x0, blocking collectives: 410 us -> none
    all_gather x2 -> x0, blocking collectives: 135 us -> none  [body(): row_actives = lax.all_gather(chosen, 'grp', axis=1, tiled=True)]
    all_to_all x0 -> x4, blocking collectives: none -> 74.7 us  [exchange(): return lax.all_to_all(value, axes, 0, 0, tiled=True)]
    slice x85 -> x0, local copies, waits for them, and re-layouts: 54.5 us -> none  [the longest x42 27.9 us: block_terms(): dvel = jpart[3:6, :, None] - iblock[3:6, None, :]]
    ppermute x14 -> x0, starting transfers between devices: 54 us -> none  [passed_along(): return lax.ppermute(value, axis, pairs)]
    pallas_call x0 -> x7, Pallas kernels: none -> 40.5 us  [call(): pl.pallas_call(kernel, out_shape=[jax.ShapeDtypeStruct(s, F32) for s in o...]
    reduce_sum x50 -> x0, other arithmetic: 27.6 us -> none  [the longest x48 27.4 us: block_terms(): accel = jnp.sum(weight[None] * dpos, axis=1)]
    mul x49 -> x0, other arithmetic: 15.3 us -> none  [the longest x48 15.3 us: block_terms(): jerk = jnp.sum(weight[None] * (dvel - radial[None] * dpos), axis=1)]
  transfers between devices with their start and end apart: 14 -> 1, of which waited for: 1 -> 0; matrix products, arithmetic and copies ran while one was open for 15% -> 0% of each run, Pallas kernels for 0% -> 18%
where the time goes in v1:
time: 128 us
  blocking collectives  74.7 us (58%)
  Pallas kernels  40.5 us (32%)
  local copies, waits for them, and re-layouts  6.13 us (5%)
  starting transfers between devices  5.66 us (4%)
    all_to_all x4, blocking collectives, exchange(): return lax.all_to_all(value, axes, 0, 0, tiled=True)  74.7 us
    pallas_call x7, Pallas kernels, call(): pl.pallas_call(kernel, out_shape=[jax.ShapeDtypeStruct(s, F32) for s in o...  40.5 us
    all_to_all x1, starting transfers between devices, exchange(): return lax.all_to_all(value, axes, 0, 0, tiled=True)  5.66 us
    unnamed x21, local copies, waits for them, and re-layouts  5.54 us
  transfers between devices with their start and end apart: 1, of which 0 were waited for; matrix products, arithmetic and copies ran while one was open for 0% of the time, Pallas kernels for 18%

profile of v1, /device:TPU:1, one launch (start us, length us, event | category | flops | bytes accessed | tf_op | source)
XLA Modules:
  0.0 127.7 jit_solution(9665290241316534208)
XLA Ops:
  0.6 0.0 copy-start
  0.6 0.7 copy.13.refs_0_
  1.4 0.0 copy-start.7
  1.4 0.0 copy-done
  1.4 0.7 copy-done.7
  2.1 0.0 copy-start.1
  2.1 0.7 copy-done.1
  2.8 0.0 copy-start.3
  2.8 0.7 copy-done.3
  3.4 0.0 copy-start.5
  3.4 0.7 copy-done.5
  4.1 0.0 copy-start.8
  4.1 0.7 copy-done.8
  4.8 0.0 copy-start.9
  4.8 0.7 copy-done.9
  5.5 1.2 shard_map.119
  6.7 17.2 %all_to_all.25.irecv = f32[32,8,128]{2,1,0:T(8,128)S(1)} all-to-all(f32[32,8,128]{2,1,0:T(8,128)S(1)} %get-tuple-element.17), channel_id=1, replica_groups=mesh['y'=4,'h'=2,'z'=16,'l'=2,'c'=2] {'y','h','l','c'}, dimensions={0} | all-to-all | bytes 262144 | tf_op jit(solution)/shard_map/all_to_all | solution.py:262
  24.0 27.3 %all_to_all.26.zrecv = f32[16,16,256]{2,1,0:T(8,128)S(1)} all-to-all(f32[16,16,256]{2,1,0:T(8,128)S(1)} %get-tuple-element.16), channel_id=1, replica_groups=mesh['y'=4,'h'=2,'z'=16,'l'=2,'c'=2] {'z'}, dimensions={0} | all-to-all | bytes 524288 | tf_op jit(solution)/shard_map/all_to_all | solution.py:262
  51.3 12.0 %shard_map.120 = (f32[32,8,384]{2,1,0:T(8,128)S(1)}, f32[16,384]{1,0:T(8,128)S(1)}, f32[8,384]{1,0:T(8,128)S(1)}, f32[256,256]{1,0:T(8,128)S(1)}) custom-call(f32[16,16,256]{2,1,0:T(8,128)S(1)} %all_to_all.26.zrecv, f32[32,8,128]{2,1,0:T(8,128)S(1)} %all_to_all.25.irecv), custom_call_target="tpu_custom_call" | custom-call | flops 62914560 | bytes 65536 | tf_op jit(solution)/shard_map/pallas_call | solution.py:250
  63.3 18.6 %all_to_all.27.precv = f32[32,8,384]{2,1,0:T(8,128)S(1)} all-to-all(f32[32,8,384]{2,1,0:T(8,128)S(1)} %get-tuple-element.18), channel_id=1, replica_groups=mesh['y'=4,'h'=2,'z'=16,'l'=2,'c'=2] {'y','h','l','c'}, dimensions={0} | all-to-all | bytes 786432 | tf_op jit(solution)/shard_map/all_to_all | solution.py:262
  81.9 0.9 shard_map.121
  82.8 5.7 %all-to-all-start.3 = ((f32[16,8,128]{2,1,0:T(8,128)}), f32[16,8,128]{2,1,0:T(8,128)S(1)}, u32[]{:S(2)}, u32[]{:S(2)}) async-start(f32[16,8,128]{2,1,0:T(8,128)} %get-tuple-element.20), calls=%async_computation.3 | async-start | bytes 131072 | tf_op jit(solution)/shard_map/all_to_all | solution.py:262
  88.5 11.8 %shard_map.123.part1 = f32[8,384]{1,0:T(8,128)S(1)} custom-call(f32[256,256]{1,0:T(8,128)S(1)} %get-tuple-element.23.jt, f32[8,384]{1,0:T(8,128)S(1)} %get-tuple-element.22.states.other), custom_call_target="tpu_custom_call" | custom-call | flops 62914560 | bytes 65536 | tf_op jit(solution)/shard_map/pallas_call | solution.py:250
  100.3 11.8 %shard_map.122.part0 = f32[8,384]{1,0:T(8,128)S(1)} custom-call(f32[256,256]{1,0:T(8,128)S(1)} %get-tuple-element.23.jt, f32[8,384]{1,0:T(8,128)S(1)} %get-tuple-element.21.states.moved), custom_call_target="tpu_custom_call" | custom-call | flops 62914560 | bytes 65536 | tf_op jit(solution)/shard_map/pallas_call | solution.py:250
  112.1 0.0 all-to-all-done.3.zrecv
  112.1 1.7 %shard_map.124 = f32[32,8,128]{2,1,0:T(8,128)S(1)} custom-call(f32[16,8,128]{2,1,0:T(8,128)S(1)} %all-to-all-done.3.zrecv, f32[8,384]{1,0:T(8,128)S(1)} %get-tuple-element.21.states.moved, f32[8,384]{1,0:T(8,128)S(1)} %get-tuple-element.22.states.other, f32[8,384]{1,0:T(8,128)S(1)} %shard_map.122.part0, f32[8,384]{1,0:T(8,128)S(1)} %shard_map.123.part1), custom_call_target="tpu_custom_call" | custom-call | flops 1000 | bytes 65536 | tf_op jit(solution)/shard_map/pallas_call | solution.py:250
  113.8 0.0 copy-start.4
  113.8 0.0 copy-start.6
  113.8 11.5 %all_to_all.28.frecv = f32[32,8,128]{2,1,0:T(8,128)S(1)} all-to-all(f32[32,8,128]{2,1,0:T(8,128)S(1)} %shard_map.124), channel_id=1, replica_groups=mesh['y'=4,'h'=2,'z'=16,'l'=2,'c'=2] {'y','h','l','c'}, dimensions={0} | all-to-all | bytes 262144 | tf_op jit(solution)/shard_map/all_to_all | solution.py:262
  125.3 0.0 copy-start.2
  125.3 0.0 copy-done.4
  125.3 0.0 copy-done.6
  125.3 0.7 copy-done.2
  126.0 1.1 shard_map.125
  127.1 0.6 copy.14
Async XLA Ops:
  0.6 0.8 copy-start
  1.4 0.7 copy-start.7
  2.1 0.7 copy-start.1
  2.8 0.7 copy-start.3
  3.4 0.7 copy-start.5
  4.1 0.7 copy-start.8
  4.8 0.7 copy-start.9
  82.8 29.3 %all-to-all-start.3 = ((f32[16,8,128]{2,1,0:T(8,128)}), f32[16,8,128]{2,1,0:T(8,128)S(1)}, u32[]{:S(2)}, u32[]{:S(2)}) async-start(f32[16,8,128]{2,1,0:T(8,128)} %get-tuple-element.20), calls=%async_computation.3 | async-start | bytes 131072 | tf_op jit(solution)/shard_map/all_to_all | solution.py:262
  113.8 11.5 %copy-start.4 = (f32[3,256]{1,0:T(4,128)S(1)}, f32[3,256]{1,0:T(4,128)}, u32[]{:S(2)}) copy-start(f32[3,256]{1,0:T(4,128)} %acc.1) | copy-start | bytes 9220
  113.8 11.5 %copy-start.6 = (f32[3,256]{1,0:T(4,128)S(1)}, f32[3,256]{1,0:T(4,128)}, u32[]{:S(2)}) copy-start(f32[3,256]{1,0:T(4,128)} %jerk.1) | copy-start | bytes 9220
  125.3 0.7 copy-start.2

commit v2 on v1

v2 whole, which is shorter than its diff:
```python
import jax
import jax.numpy as jnp
from jax import lax
from jax.experimental import pallas as pl
from jax.experimental.pallas import tpu as pltpu
from jax.sharding import Mesh, PartitionSpec as P

STEP_BASE = 0.125
SOFTEN = 0.01
PART = 256
SLOTS = 24
CHIPS = 16
PLANE = 2 * CHIPS
COLUMN = 16
COLS = SLOTS * CHIPS
SHARE = SLOTS // 2
LANES = 128
LISTED = 32
RATES = 64
ALL_AXES = ("y", "h", "z", "l", "c")
PLANE_AXES = ("y", "h", "l", "c")
EXACT = lax.Precision.HIGHEST
F32 = jnp.float32
I32 = jnp.int32
BF16 = jnp.bfloat16
NT = (((1,), (1,)), ((), ()))
TN = (((0,), (0,)), ((), ()))


def predict(pos, vel, acc, jerk, elapsed):
    pred_pos = pos + elapsed * (vel + elapsed * (acc * 0.5 + elapsed * jerk / 6.0))
    pred_vel = vel + elapsed * (acc + elapsed * jerk * 0.5)
    return (pred_pos, pred_vel)


def correct(pos, vel, acc, jerk, new_acc, new_jerk, stride):
    half = 0.5 * stride
    square = stride * stride / 12.0
    vel_new = vel + half * (acc + new_acc) + square * (jerk - new_jerk)
    pos_new = pos + half * (vel + vel_new) + square * (acc - new_acc)
    return (pos_new, vel_new)


def iota(shape, axis):
    return lax.broadcasted_iota(I32, shape, axis)


def prepare_kernel(
    total, pos_h, vel_h, acc_h, jerk_h, weight_h, lev_h, active_h, counts_h, zsend, isend, place, slots, keep,
    jrows, srows, state, weight, levels, active, counts, sems,
):
    copies = [
        pltpu.make_async_copy(src, dst, sems.at[k])
        for k, (src, dst) in enumerate(
            (
                (pos_h, state.at[0]),
                (vel_h, state.at[1]),
                (acc_h, state.at[2]),
                (jerk_h, state.at[3]),
                (weight_h, weight),
                (lev_h, levels),
                (active_h, active),
                (counts_h, counts),
            )
        )
    ]
    for copy in copies:
        copy.start()
    for copy in copies:
        copy.wait()
    core = lax.axis_index("c")
    mass = weight[...] / total
    lev = levels[...]
    p, v, a, j = state[0], state[1], state[2], state[3]
    p1, v1 = predict(p, v, a, j, STEP_BASE)
    p2, v2 = predict(p, v, a, j, 2 * STEP_BASE)
    for k, part in enumerate((p, v, a, j)):
        keep[3 * k : 3 * k + 3] = part
    keep[12:13] = lev.astype(F32)
    keep[13:16] = jnp.zeros((3, PART), F32)
    jrows[0:3] = p1
    jrows[3:6] = v1
    jrows[6:7] = mass
    jrows[7:8] = jnp.zeros((1, PART), F32)
    jrows[8:11] = p2
    jrows[11:14] = v2
    jrows[14:15] = jnp.where(lev == 0, 0.0, mass)
    jrows[15:16] = jnp.zeros((1, PART), F32)
    rows = jrows[...]
    for k in range(COLUMN):
        zsend[k] = rows
    srows[...] = jnp.zeros(srows.shape, F32)
    srows[0:3] = p
    srows[3:6] = v
    srows[6:7] = mass
    srows[8:11] = p2
    srows[11:14] = v2
    srows[16:19] = a
    srows[19:22] = j

    n1, n2 = counts[0:1, 0:1], counts[0:1, 1:2]
    off0 = jnp.where(core == 1, SLOTS - n1, 0)
    off1 = jnp.where(core == 1, n1, 0)
    who = iota((PART, SLOTS), 0)
    slot = iota((PART, SLOTS), 1)
    a1 = ((who == active[0:1, :]) & (slot < n1)).astype(F32)
    a2 = ((who == active[1:2, :]) & (slot < n2)).astype(F32)
    col = iota((LANES, SLOTS), 0)
    cslot = iota((LANES, SLOTS), 1)
    first = (col == cslot + off0) & (cslot < n1)
    again = (col == cslot + off0 + RATES) & (cslot < n1)
    first_f = first.astype(F32)
    listed = jnp.dot(jnp.broadcast_to(lev.astype(F32), (8, PART)), a2, preferred_element_type=F32)
    live = iota((8, SLOTS), 1) < n2
    is0 = (live & (listed < 0.5)).astype(F32)
    is1 = (live & (listed > 0.5) & (listed < 1.5)).astype(F32)
    before = (iota((SLOTS, SLOTS), 0) < iota((SLOTS, SLOTS), 1)).astype(F32)
    rank0 = jnp.dot(is0, before, preferred_element_type=F32)[0:1].astype(I32)
    rank1 = jnp.dot(is1, before, preferred_element_type=F32)[0:1].astype(I32)
    second = ((col == rank1 + (off1 + LISTED)) & (is1[0:1] > 0.5)).astype(F32)
    held = ((col == rank0 + off0) & (is0[0:1] > 0.5)).astype(F32)
    spots = lax.dot_general(a1, first_f + again.astype(F32), NT, preferred_element_type=F32)
    spots = spots + lax.dot_general(a2, second, NT, preferred_element_type=F32)
    place[...] = spots
    slots[0] = first_f
    slots[1] = held + second
    picked = jnp.dot(srows[...], spots, precision=EXACT, preferred_element_type=F32)
    lane = iota((8, LANES), 1)
    payload = jnp.where(lane < LISTED, picked[0:8], jnp.where(lane < RATES, picked[8:16], picked[16:24]))
    for k in range(PLANE):
        isend[k] = payload


def rounded(value):
    return value.astype(BF16).astype(F32)


def split(value):
    high = rounded(value)
    middle = rounded(value - high)
    return high, middle, value - high - middle


def source_parts(rows, feats, values):
    count = rows.shape[0]
    row = iota(rows.shape, 0) % 8

    def ahead(value, by):
        return pltpu.roll(value, (count - by) % count, 0)

    square = rows * rows
    square = square + ahead(square, 1) + ahead(square, 2)
    cross = rows * ahead(rows, 3)
    cross = cross + ahead(cross, 1) + ahead(cross, 2)
    full = jnp.where(row == 6, 1.0, jnp.where(row == 7, ahead(square, count - 7), rows))
    high, middle, low = split(full)
    c_high, c_middle, c_low = split(cross)
    c_rows = jnp.where(row == 1, ahead(c_middle, count - 1), jnp.where(row == 2, ahead(c_low, count - 2), 0.0))
    c_rows = jnp.where(row == 0, c_high, c_rows)
    blank = jnp.zeros((8, PART), F32)
    for k in range(count // 8):
        here, cols = slice(8 * k, 8 * k + 8), slice(PART * k, PART * (k + 1))
        h, m, low_k = high[here], middle[here], low[here]
        feats[:, cols] = jnp.concatenate([h, h, m, m, h, low_k, c_rows[here], blank], axis=0).astype(BF16)
        weighed = rows[8 * k + 6 : 8 * k + 7] * jnp.where(row[here] == 6, 1.0, rows[here])
        weighed = jnp.where(row[here] == 7, 0.0, weighed)
        values[:, cols] = jnp.concatenate([*split(weighed), blank], axis=0).astype(BF16)


def target_parts(states):
    row = iota(states.shape, 0)
    square = states[0:3] * states[0:3]
    square = square[0:1] + square[1:2] + square[2:3] + SOFTEN
    cross = states[0:3] * states[3:6]
    cross = cross[0:1] + cross[1:2] + cross[2:3]
    turned = jnp.concatenate([states[3:6], states[0:3], states[6:8]], axis=0)
    near = jnp.where(row < 3, -2.0 * states, jnp.where(row < 6, 0.0, jnp.where(row == 6, square, 1.0)))
    rate = jnp.where(row < 6, -turned, jnp.where(row == 6, cross, 0.0))
    parts = []
    for full, one in ((near, 0.0), (rate, 1.0)):
        h, m, low = split(full)
        unit = jnp.where(row < 3, one, 0.0)
        parts.append(jnp.concatenate([h, m, h, m, low, h, unit, jnp.zeros_like(unit)], axis=0).astype(BF16))
    return parts


def pair_sums(states, feats, values, width):
    near, rate = target_parts(states)
    sum_w = sum_u = None
    for k in range(feats.shape[1] // width):
        cols = slice(width * k, width * (k + 1))
        feat, value = feats[:, cols], values[:, cols]
        dist = lax.dot_general(feat, near, TN, preferred_element_type=F32)
        radial = lax.dot_general(feat, rate, TN, preferred_element_type=F32)
        inv = lax.rsqrt(jnp.maximum(dist, SOFTEN))
        inv2 = inv * inv
        w = inv * inv2
        u = w * inv2 * radial
        total = []
        for term in (w, u):
            high = term.astype(BF16)
            low = (term - high.astype(F32)).astype(BF16)
            total.append(
                jnp.dot(value, high, preferred_element_type=F32) + jnp.dot(value, low, preferred_element_type=F32)
            )
        sum_w = total[0] if k == 0 else sum_w + total[0]
        sum_u = total[1] if k == 0 else sum_u + total[1]
    w = sum_w[0:8] + sum_w[8:16] + sum_w[16:24]
    u = sum_u[0:8] + sum_u[8:16] + sum_u[16:24]
    acc = w[0:3] - states[0:3] * w[6:7]
    jerk = w[3:6] - states[3:6] * w[6:7] - 3.0 * (u[0:3] - states[0:3] * u[6:7])
    return jnp.concatenate([acc, jerk, jnp.zeros((2, states.shape[1]), F32)], axis=0)


def first_kernel(zrecv, irecv, psend, known, other, feats, values):
    for q in range(CHIPS):
        block = irecv[2 * q] + irecv[2 * q + 1]
        here = slice(SLOTS * q, SLOTS * (q + 1))
        known[0:8, here] = block[:, 0:SLOTS]
        known[8:16, here] = block[:, RATES : RATES + SLOTS]
        other[:, here] = block[:, LISTED : LISTED + SLOTS]
    source_parts(zrecv[:, 0:8, :].reshape(8 * COLUMN, PART), feats, values)
    p1, v1 = predict(known[0:3], known[3:6], known[8:11], known[11:14], STEP_BASE)
    states = jnp.concatenate([p1, v1, jnp.zeros((2, COLS), F32)], axis=0)
    part = pair_sums(states, feats, values, 8 * PART)
    for k in range(PLANE):
        psend[k] = part


def later_kernel(zrecv, moved, other, out, feats, values):
    source_parts(zrecv[:, 8:16, :].reshape(8 * COLUMN, PART), feats, values)
    out[...] = pair_sums(jnp.concatenate([moved[...], other[...]], axis=1), feats, values, 4 * PART)


def update_kernel(precv, known, zsend, moved, mine):
    total = precv[0]
    for k in range(1, PLANE):
        total = total + precv[k]
    p, v, a, j = known[0:3], known[3:6], known[8:11], known[11:14]
    new_a, new_j = total[0:3], total[3:6]
    pos, vel = correct(p, v, a, j, new_a, new_j, STEP_BASE)
    p2, v2 = predict(pos, vel, new_a, new_j, STEP_BASE)
    moved[0:3] = p2
    moved[3:6] = v2
    moved[6:7] = known[6:7]
    moved[7:8] = jnp.zeros((1, COLS), F32)
    chip = (lax.axis_index("y") * 2 + lax.axis_index("h")) * 2 + lax.axis_index("l")
    core = lax.axis_index("c")
    spot = lax.rem(lax.axis_index("z"), 8) * 16
    row = iota((COLS, LANES), 0)
    lane = iota((COLS, LANES), 1)
    index = lane - spot
    share = ((row == index + (chip * SLOTS + core * SHARE)) & (index >= 0) & (index < SHARE)).astype(F32)
    block = ((row == lane + chip * SLOTS) & (lane < SLOTS)).astype(F32)
    payload = jnp.dot(moved[...], share, precision=EXACT, preferred_element_type=F32)
    for k in range(COLUMN):
        zsend[k] = payload
    mine[...] = jnp.dot(total, block, precision=EXACT, preferred_element_type=F32)


def last_kernel(zrecv, moved, other, part, fsend, feats, values, sums):
    halves = []
    for base in (0, 8):
        half = zrecv[base]
        for k in range(1, 8):
            half = half + zrecv[base + k]
        halves.append(half)
    source_parts(jnp.concatenate(halves, axis=1), feats, values)
    states = jnp.concatenate([moved[...], other[...]], axis=1)
    sums[...] = pair_sums(states, feats, values, PART) + part[...]
    for q in range(CHIPS):
        here = slice(SLOTS * q, SLOTS * (q + 1))
        there = slice(COLS + SLOTS * q, COLS + SLOTS * (q + 1))
        for k in (2 * q, 2 * q + 1):
            fsend[k] = jnp.zeros((8, LANES), F32)
            fsend[k, :, 0:SLOTS] = sums[:, here]
            fsend[k, :, LISTED : LISTED + SLOTS] = sums[:, there]


def finish_kernel(keep, frecv, mine, place, slots, pos_o, vel_o, acc_o, jerk_o, fresh):
    total = frecv[0]
    for k in range(1, PLANE):
        total = total + frecv[k]
    once = mine[...]
    fresh[:, 0, :] = jnp.dot(once, slots[0], precision=EXACT, preferred_element_type=F32)[0:6]
    fresh[:, 1, :] = jnp.dot(total, slots[1], precision=EXACT, preferred_element_type=F32)[0:6]
    lane = iota((8, LANES), 1)
    spots = place[...]
    spread = [
        lax.dot_general(jnp.where(lane < RATES, value, 0.0), spots, NT, precision=EXACT, preferred_element_type=F32)
        for value in (once, total)
    ]
    lev = keep[12:13].astype(I32)
    stride = STEP_BASE * jnp.left_shift(jnp.ones_like(lev), lev).astype(F32)
    p, v, a, j = keep[0:3], keep[3:6], keep[6:9], keep[9:12]
    for step in range(2):
        new_a, new_j = spread[step][0:3], spread[step][3:6]
        hit = lev <= step
        p_new, v_new = correct(p, v, a, j, new_a, new_j, stride)
        p, v = jnp.where(hit, p_new, p), jnp.where(hit, v_new, v)
        a, j = jnp.where(hit, new_a, a), jnp.where(hit, new_j, j)
    pos_o[...] = p
    vel_o[...] = v
    acc_o[...] = a
    jerk_o[...] = j


def call(kernel, ins, outs, scratch=(), far=0, mib=8):
    vmem = pl.BlockSpec(memory_space=pltpu.VMEM)
    return pl.pallas_call(
        kernel,
        out_shape=[jax.ShapeDtypeStruct(s, F32) for s in outs],
        in_specs=[pl.BlockSpec(memory_space=pltpu.HBM)] * far + [vmem] * (len(ins) - far),
        out_specs=[vmem] * len(outs),
        scratch_shapes=list(scratch),
        compiler_params=pltpu.CompilerParams(vmem_limit_bytes=mib * 1024 * 1024),
    )(*ins)


def operands(sources):
    return [pltpu.VMEM((64, sources), BF16), pltpu.VMEM((32, sources), BF16)]


def exchange(value, axes):
    return lax.all_to_all(value, axes, 0, 0, tiled=True)


def body(positions, velocities, accelerations, jerks, mass_weight, levels, active, counts):
    total_part = PART * lax.axis_size(ALL_AXES)
    lev = levels.reshape(1, PART)
    state = (positions, velocities, accelerations, jerks)

    def prepare(*refs):
        prepare_kernel(total_part, *refs)

    zsend, isend, place, slots, keep = call(
        prepare,
        (*state, mass_weight.reshape(1, PART), lev, active, counts.reshape(1, 2)),
        [(COLUMN, 16, PART), (PLANE, 8, LANES), (PART, LANES), (2, LANES, SLOTS), (16, PART)],
        [
            pltpu.VMEM((16, PART), F32),
            pltpu.VMEM((24, PART), F32),
            pltpu.VMEM((4, 3, PART), F32),
            pltpu.VMEM((1, PART), F32),
            pltpu.VMEM((1, PART), I32),
            pltpu.VMEM((2, SLOTS), I32),
            pltpu.VMEM((1, 2), I32),
            pltpu.SemaphoreType.DMA((8,)),
        ],
        far=8,
        mib=60,
    )
    irecv = exchange(isend, PLANE_AXES)
    zrecv = exchange(zsend, "z")
    psend, known, other = call(
        first_kernel, (zrecv, irecv), [(PLANE, 8, COLS), (16, COLS), (8, COLS)], operands(COLUMN * PART), mib=24
    )
    precv = exchange(psend, PLANE_AXES)
    zsend2, moved, mine = call(update_kernel, (precv, known), [(COLUMN, 8, LANES), (8, COLS), (8, LANES)])
    zrecv2 = exchange(zsend2, "z")
    (part,) = call(later_kernel, (zrecv, moved, other), [(8, 2 * COLS)], operands(COLUMN * PART), mib=24)
    (fsend,) = call(
        last_kernel,
        (zrecv2, moved, other, part),
        [(PLANE, 8, LANES)],
        operands(PART) + [pltpu.VMEM((8, 2 * COLS), F32)],
    )
    frecv = exchange(fsend, PLANE_AXES)
    *state, fresh = call(
        finish_kernel,
        (keep, frecv, mine, place, slots),
        [(3, PART)] * 4 + [(6, 2, SLOTS)],
    )
    return (*state, fresh.transpose(1, 0, 2))


def solution(mesh):
    fine = Mesh(mesh.devices.reshape(4, 2, 16, 2, 2), ALL_AXES)
    rows, flat = P(None, ALL_AXES), P(ALL_AXES)
    in_specs = (rows, rows, rows, rows, flat, flat, rows, rows)
    out_specs = (rows, rows, rows, rows, P(None, None, ALL_AXES))
    return jax.shard_map(body, mesh=fine, in_specs=in_specs, out_specs=out_specs, check_vma=False)
```

time: 128 us -> 105 us (0.82)
  Pallas kernels: 40.5 us -> 18.8 us
  local copies, waits for them, and re-layouts: 6.13 us -> 0.02 us
  waiting for transfers between devices: 0.01 us -> 2.7 us
  blocking collectives: 74.7 us -> 76.3 us
    pallas_call x7 -> x6, Pallas kernels: 40.5 us -> 18.8 us  [call(): pl.pallas_call(kernel, out_shape=[jax.ShapeDtypeStruct(s, F32) for s in o...]
    unnamed x21 -> x8, local copies, waits for them, and re-layouts: 5.54 us -> 0.02 us
    all_to_all x1, waiting for transfers between devices: 0.01 us -> 2.7 us  [exchange(): return lax.all_to_all(value, axes, 0, 0, tiled=True)]
    all_to_all x4, blocking collectives: 74.7 us -> 76.3 us  [exchange(): return lax.all_to_all(value, axes, 0, 0, tiled=True)]
  transfers between devices with their start and end apart: 1 -> 1, of which waited for: 0 -> 1; matrix products, arithmetic and copies ran while one was open for 0% -> 0% of each run, Pallas kernels for 18% -> 9%
where the time goes in v2:
time: 105 us; the launch traced here: 104 us
  blocking collectives  76.3 us (73%)
  Pallas kernels  18.8 us (18%)
  starting transfers between devices  5.67 us (5%)
  waiting for transfers between devices  2.7 us (3%)
    all_to_all x4, blocking collectives, exchange(): return lax.all_to_all(value, axes, 0, 0, tiled=True)  76.3 us
    pallas_call x6, Pallas kernels, call(): pl.pallas_call(kernel, out_shape=[jax.ShapeDtypeStruct(s, F32) for s in o...  18.8 us
    all_to_all x1, starting transfers between devices, exchange(): return lax.all_to_all(value, axes, 0, 0, tiled=True)  5.67 us
    all_to_all x1, waiting for transfers between devices, exchange(): return lax.all_to_all(value, axes, 0, 0, tiled=True)  2.7 us
  transfers between devices with their start and end apart: 1, of which 1 were waited for; matrix products, arithmetic and copies ran while one was open for 0% of the time, Pallas kernels for 9%

profile of v2, /device:TPU:1, one launch (start us, length us, event | category | flops | bytes accessed | tf_op | source)
XLA Modules:
  0.0 104.3 jit_solution(11891869778075328592)
XLA Ops:
  0.6 2.3 %shard_map.119 = (f32[16,16,256]{2,1,0:T(8,128)}, f32[32,8,128]{2,1,0:T(8,128)}, f32[256,128]{1,0:T(8,128)}, f32[2,128,24]{2,1,0:T(8,128)}, f32[16,256]{1,0:T(8,128)}) custom-call(f32[3,256]{1,0:T(4,128)} %refs_0_.1, f32[3,256]{1,0:T(4,128)} %refs_1_.1, f32[3,256]{1,0:T(4,128)} %refs_2_.1, f32[3,256]{1,0:T(4,128)} %refs_3_.1, f32[1,256]{1,0:T(1,128)} %bitcast.4, ...), custom_call_target="tpu_custom_call" | custom-call | tf_op jit(solution)/shard_map/pallas_call | solution.py:310
  2.9 0.0 copy-start.3
  2.9 18.2 %all_to_all.25.irecv = f32[32,8,128]{2,1,0:T(8,128)S(1)} all-to-all(f32[32,8,128]{2,1,0:T(8,128)} %get-tuple-element.23), channel_id=1, replica_groups=mesh['y'=4,'h'=2,'z'=16,'l'=2,'c'=2] {'y','h','l','c'}, dimensions={0} | all-to-all | bytes 262144 | tf_op jit(solution)/shard_map/all_to_all | solution.py:325
  21.2 0.0 copy-done.3
  21.2 26.7 %all_to_all.26.zrecv = f32[16,16,256]{2,1,0:T(8,128)S(1)} all-to-all(f32[16,16,256]{2,1,0:T(8,128)S(1)} %copy-done.3), channel_id=1, replica_groups=mesh['y'=4,'h'=2,'z'=16,'l'=2,'c'=2] {'z'}, dimensions={0} | all-to-all | bytes 524288 | tf_op jit(solution)/shard_map/all_to_all | solution.py:325
  47.9 4.7 %shard_map.120 = (f32[32,8,384]{2,1,0:T(8,128)S(1)}, f32[16,384]{1,0:T(8,128)S(1)}, f32[8,384]{1,0:T(8,128)S(1)}) custom-call(f32[16,16,256]{2,1,0:T(8,128)S(1)} %all_to_all.26.zrecv, f32[32,8,128]{2,1,0:T(8,128)S(1)} %all_to_all.25.irecv), custom_call_target="tpu_custom_call" | custom-call | tf_op jit(solution)/shard_map/pallas_call | solution.py:310
  52.6 18.6 %all_to_all.27.precv = f32[32,8,384]{2,1,0:T(8,128)S(1)} all-to-all(f32[32,8,384]{2,1,0:T(8,128)S(1)} %get-tuple-element.24), channel_id=1, replica_groups=mesh['y'=4,'h'=2,'z'=16,'l'=2,'c'=2] {'y','h','l','c'}, dimensions={0} | all-to-all | bytes 786432 | tf_op jit(solution)/shard_map/all_to_all | solution.py:325
  71.2 0.9 shard_map.121
  72.1 5.7 %all-to-all-start.3 = ((f32[16,8,128]{2,1,0:T(8,128)}), f32[16,8,128]{2,1,0:T(8,128)S(1)}, u32[]{:S(2)}, u32[]{:S(2)}) async-start(f32[16,8,128]{2,1,0:T(8,128)} %get-tuple-element.26), calls=%async_computation.3 | async-start | bytes 131072 | tf_op jit(solution)/shard_map/all_to_all | solution.py:325
  77.8 9.0 %shard_map.122.part = f32[8,768]{1,0:T(8,128)S(1)} custom-call(f32[16,16,256]{2,1,0:T(8,128)S(1)} %all_to_all.26.zrecv, f32[8,384]{1,0:T(8,128)S(1)} %get-tuple-element.27.moved, f32[8,384]{1,0:T(8,128)S(1)} %get-tuple-element.28.other), custom_call_target="tpu_custom_call" | custom-call | tf_op jit(solution)/shard_map/pallas_call | solution.py:310
  86.8 2.7 %all-to-all-done.3.zrecv = f32[16,8,128]{2,1,0:T(8,128)S(1)} async-done(((f32[16,8,128]{2,1,0:T(8,128)}), f32[16,8,128]{2,1,0:T(8,128)S(1)}, u32[]{:S(2)}, u32[]{:S(2)}) %all-to-all-start.3) | async-done | bytes 65568 | tf_op jit(solution)/shard_map/all_to_all | solution.py:325
  89.5 0.0 copy-start.2
  89.5 0.9 shard_map.123
  90.3 0.0 copy-start
  90.4 0.0 copy-start.1
  90.4 12.8 %all_to_all.28.frecv = f32[32,8,128]{2,1,0:T(8,128)S(1)} all-to-all(f32[32,8,128]{2,1,0:T(8,128)S(1)} %shard_map.123), channel_id=1, replica_groups=mesh['y'=4,'h'=2,'z'=16,'l'=2,'c'=2] {'y','h','l','c'}, dimensions={0} | all-to-all | bytes 262144 | tf_op jit(solution)/shard_map/all_to_all | solution.py:325
  103.2 0.0 copy-done.2
  103.2 0.0 copy-done
  103.2 0.0 copy-done.1
  103.2 1.1 %shard_map.124 = (f32[3,256]{1,0:T(4,128)}, f32[3,256]{1,0:T(4,128)}, f32[3,256]{1,0:T(4,128)}, f32[3,256]{1,0:T(4,128)}, f32[6,2,24]{2,1,0:T(2,128)}) custom-call(f32[16,256]{1,0:T(8,128)S(1)} %copy-done.2, f32[32,8,128]{2,1,0:T(8,128)S(1)} %all_to_all.28.frecv, f32[8,128]{1,0:T(8,128)S(1)} %get-tuple-element.29.mine, f32[256,128]{1,0:T(8,128)S(1)} %copy-done, ...), custom_call_target="tpu_custom_call" | custom-call | tf_op jit(solution)/shard_map/pallas_call | solution.py:310
Async XLA Ops:
  2.9 18.3 %copy-start.3 = (f32[16,16,256]{2,1,0:T(8,128)S(1)}, f32[16,16,256]{2,1,0:T(8,128)}, u32[]{:S(2)}) copy-start(f32[16,16,256]{2,1,0:T(8,128)} %get-tuple-element.22) | copy-start | bytes 786436
  72.1 17.4 %all-to-all-start.3 = ((f32[16,8,128]{2,1,0:T(8,128)}), f32[16,8,128]{2,1,0:T(8,128)S(1)}, u32[]{:S(2)}, u32[]{:S(2)}) async-start(f32[16,8,128]{2,1,0:T(8,128)} %get-tuple-element.26), calls=%async_computation.3 | async-start | bytes 131072 | tf_op jit(solution)/shard_map/all_to_all | solution.py:325
  89.5 13.7 %copy-start.2 = (f32[16,256]{1,0:T(8,128)S(1)}, f32[16,256]{1,0:T(8,128)}, u32[]{:S(2)}) copy-start(f32[16,256]{1,0:T(8,128)} %get-tuple-element.21.keep) | copy-start | bytes 49156
  90.3 12.8 %copy-start = (f32[256,128]{1,0:T(8,128)S(1)}, f32[256,128]{1,0:T(8,128)}, u32[]{:S(2)}) copy-start(f32[256,128]{1,0:T(8,128)} %get-tuple-element.30.place) | copy-start | bytes 393220
  90.4 12.8 %copy-start.1 = (f32[2,128,24]{2,1,0:T(8,128)S(1)}, f32[2,128,24]{2,1,0:T(8,128)}, u32[]{:S(2)}) copy-start(f32[2,128,24]{2,1,0:T(8,128)} %get-tuple-element.31.slots) | copy-start | bytes 73732

commit v3 on v2

--- a/solution.py
+++ b/solution.py
@@ -17,8 +17,9 @@
 LANES = 128
 LISTED = 32
 RATES = 64
-ALL_AXES = ("y", "h", "z", "l", "c")
-PLANE_AXES = ("y", "h", "l", "c")
+ALL_AXES = ("a", "b", "h", "z", "l", "c")
+PLANE_AXES = ("a", "b", "h", "l", "c")
+STAGES = (("l", "c"), "h", "b", "a")
 EXACT = lax.Precision.HIGHEST
 F32 = jnp.float32
 I32 = jnp.int32
@@ -127,8 +128,7 @@
     picked = jnp.dot(srows[...], spots, precision=EXACT, preferred_element_type=F32)
     lane = iota((8, LANES), 1)
     payload = jnp.where(lane < LISTED, picked[0:8], jnp.where(lane < RATES, picked[8:16], picked[16:24]))
-    for k in range(PLANE):
-        isend[k] = payload
+    isend[...] = payload
 
 
 def rounded(value):
@@ -185,26 +185,22 @@
 
 
 def pair_sums(states, feats, values, width):
-    near, rate = target_parts(states)
-    sum_w = sum_u = None
+    count = states.shape[1]
+    both = jnp.concatenate(target_parts(states), axis=1)
+    total = None
     for k in range(feats.shape[1] // width):
         cols = slice(width * k, width * (k + 1))
-        feat, value = feats[:, cols], values[:, cols]
-        dist = lax.dot_general(feat, near, TN, preferred_element_type=F32)
-        radial = lax.dot_general(feat, rate, TN, preferred_element_type=F32)
-        inv = lax.rsqrt(jnp.maximum(dist, SOFTEN))
+        product = lax.dot_general(feats[:, cols], both, TN, preferred_element_type=F32)
+        inv = lax.rsqrt(jnp.maximum(product[:, :count], SOFTEN))
         inv2 = inv * inv
         w = inv * inv2
-        u = w * inv2 * radial
-        total = []
-        for term in (w, u):
-            high = term.astype(BF16)
-            low = (term - high.astype(F32)).astype(BF16)
-            total.append(
-                jnp.dot(value, high, preferred_element_type=F32) + jnp.dot(value, low, preferred_element_type=F32)
-            )
-        sum_w = total[0] if k == 0 else sum_w + total[0]
-        sum_u = total[1] if k == 0 else sum_u + total[1]
+        terms = (w, w * inv2 * product[:, count:])
+        high = [term.astype(BF16) for term in terms]
+        low = [(term - part.astype(F32)).astype(BF16) for term, part in zip(terms, high)]
+        for part in (high, low):
+            term = jnp.dot(values[:, cols], jnp.concatenate(part, axis=1), preferred_element_type=F32)
+            total = term if total is None else total + term
+    sum_w, sum_u = total[:, :count], total[:, count:]
     w = sum_w[0:8] + sum_w[8:16] + sum_w[16:24]
     u = sum_u[0:8] + sum_u[8:16] + sum_u[16:24]
     acc = w[0:3] - states[0:3] * w[6:7]
@@ -223,19 +219,24 @@
     p1, v1 = predict(known[0:3], known[3:6], known[8:11], known[11:14], STEP_BASE)
     states = jnp.concatenate([p1, v1, jnp.zeros((2, COLS), F32)], axis=0)
     part = pair_sums(states, feats, values, 8 * PART)
+    halves = [jnp.concatenate([part[3 * row + k : 3 * row + k + 1] for k in range(3)], axis=1) for row in range(2)]
+    both = jnp.concatenate(halves, axis=0)
     for k in range(PLANE):
-        psend[k] = part
+        psend[k] = both
 
 
 def later_kernel(zrecv, moved, other, out, feats, values):
     source_parts(zrecv[:, 8:16, :].reshape(8 * COLUMN, PART), feats, values)
-    out[...] = pair_sums(jnp.concatenate([moved[...], other[...]], axis=1), feats, values, 4 * PART)
+    out[:, 0:COLS] = pair_sums(moved[...], feats, values, 8 * PART)
+    out[:, COLS:] = pair_sums(other[...], feats, values, 8 * PART)
 
 
 def update_kernel(precv, known, zsend, moved, mine):
-    total = precv[0]
+    both = precv[0]
     for k in range(1, PLANE):
-        total = total + precv[k]
+        both = both + precv[k]
+    total = [both[row : row + 1, COLS * k : COLS * (k + 1)] for row in range(2) for k in range(3)]
+    total = jnp.concatenate([*total, jnp.zeros((2, COLS), F32)], axis=0)
     p, v, a, j = known[0:3], known[3:6], known[8:11], known[11:14]
     new_a, new_j = total[0:3], total[3:6]
     pos, vel = correct(p, v, a, j, new_a, new_j, STEP_BASE)
@@ -244,28 +245,33 @@
     moved[3:6] = v2
     moved[6:7] = known[6:7]
     moved[7:8] = jnp.zeros((1, COLS), F32)
-    chip = (lax.axis_index("y") * 2 + lax.axis_index("h")) * 2 + lax.axis_index("l")
+    chip = lax.axis_index("a")
+    for axis in ("b", "h", "l"):
+        chip = chip * 2 + lax.axis_index(axis)
     core = lax.axis_index("c")
-    spot = lax.rem(lax.axis_index("z"), 8) * 16
     row = iota((COLS, LANES), 0)
     lane = iota((COLS, LANES), 1)
-    index = lane - spot
-    share = ((row == index + (chip * SLOTS + core * SHARE)) & (index >= 0) & (index < SHARE)).astype(F32)
+    index = lane % 16
+    share = ((row == index + (chip * SLOTS + core * SHARE)) & (index < SHARE)).astype(F32)
     block = ((row == lane + chip * SLOTS) & (lane < SLOTS)).astype(F32)
     payload = jnp.dot(moved[...], share, precision=EXACT, preferred_element_type=F32)
+    payload = jnp.where(iota((8, LANES), 0) == iota((8, LANES), 1) // 16, payload, 0.0)
+    payload = jnp.sum(payload, axis=0, keepdims=True)
     for k in range(COLUMN):
         zsend[k] = payload
     mine[...] = jnp.dot(total, block, precision=EXACT, preferred_element_type=F32)
 
 
-def last_kernel(zrecv, moved, other, part, fsend, feats, values, sums):
-    halves = []
-    for base in (0, 8):
-        half = zrecv[base]
-        for k in range(1, 8):
-            half = half + zrecv[base + k]
-        halves.append(half)
-    source_parts(jnp.concatenate(halves, axis=1), feats, values)
+def last_kernel(zrecv, moved, other, part, fsend, feats, values, rows, sums):
+    lane = iota((8, LANES), 1)
+    rows[...] = jnp.zeros(rows.shape, F32)
+    for half in range(2):
+        packed = zrecv[8 * half : 8 * half + 8, 0, :]
+        for k in range(7):
+            item = jnp.where(lane < 16, pltpu.roll(packed, (LANES - 16 * k) % LANES, 1), 0.0)
+            item = pltpu.roll(item, 0, 1, stride=16, stride_axis=0)
+            rows[k : k + 1, LANES * half : LANES * (half + 1)] = jnp.sum(item, axis=0, keepdims=True)
+    source_parts(rows[...], feats, values)
     states = jnp.concatenate([moved[...], other[...]], axis=1)
     sums[...] = pair_sums(states, feats, values, PART) + part[...]
     for q in range(CHIPS):
@@ -321,6 +327,12 @@
     return [pltpu.VMEM((64, sources), BF16), pltpu.VMEM((32, sources), BF16)]
 
 
+def gathered(value):
+    for axes in STAGES:
+        value = lax.all_gather(value, axes, tiled=True)
+    return value.reshape(PLANE, 8, LANES)
+
+
 def exchange(value, axes):
     return lax.all_to_all(value, axes, 0, 0, tiled=True)
 
@@ -336,7 +348,7 @@
     zsend, isend, place, slots, keep = call(
         prepare,
         (*state, mass_weight.reshape(1, PART), lev, active, counts.reshape(1, 2)),
-        [(COLUMN, 16, PART), (PLANE, 8, LANES), (PART, LANES), (2, LANES, SLOTS), (16, PART)],
+        [(COLUMN, 16, PART), (8, LANES), (PART, LANES), (2, LANES, SLOTS), (16, PART)],
         [
             pltpu.VMEM((16, PART), F32),
             pltpu.VMEM((24, PART), F32),
@@ -350,20 +362,20 @@
         far=8,
         mib=60,
     )
-    irecv = exchange(isend, PLANE_AXES)
+    irecv = gathered(isend)
     zrecv = exchange(zsend, "z")
     psend, known, other = call(
-        first_kernel, (zrecv, irecv), [(PLANE, 8, COLS), (16, COLS), (8, COLS)], operands(COLUMN * PART), mib=24
+        first_kernel, (zrecv, irecv), [(PLANE, 2, 3 * COLS), (16, COLS), (8, COLS)], operands(COLUMN * PART), mib=24
     )
     precv = exchange(psend, PLANE_AXES)
-    zsend2, moved, mine = call(update_kernel, (precv, known), [(COLUMN, 8, LANES), (8, COLS), (8, LANES)])
+    zsend2, moved, mine = call(update_kernel, (precv, known), [(COLUMN, 1, LANES), (8, COLS), (8, LANES)])
     zrecv2 = exchange(zsend2, "z")
     (part,) = call(later_kernel, (zrecv, moved, other), [(8, 2 * COLS)], operands(COLUMN * PART), mib=24)
     (fsend,) = call(
         last_kernel,
         (zrecv2, moved, other, part),
         [(PLANE, 8, LANES)],
-        operands(PART) + [pltpu.VMEM((8, 2 * COLS), F32)],
+        operands(PART) + [pltpu.VMEM((8, PART), F32), pltpu.VMEM((8, 2 * COLS), F32)],
     )
     frecv = exchange(fsend, PLANE_AXES)
     *state, fresh = call(
@@ -375,7 +387,7 @@
 
 
 def solution(mesh):
-    fine = Mesh(mesh.devices.reshape(4, 2, 16, 2, 2), ALL_AXES)
+    fine = Mesh(mesh.devices.reshape(2, 2, 2, 16, 2, 2), ALL_AXES)
     rows, flat = P(None, ALL_AXES), P(ALL_AXES)
     in_specs = (rows, rows, rows, rows, flat, flat, rows, rows)
     out_specs = (rows, rows, rows, rows, P(None, None, ALL_AXES))

time: 105 us -> 101 us (0.962)
  blocking collectives: 76.3 us -> 51.8 us
  starting transfers between devices: 5.67 us -> 27.5 us
    all_to_all x4 -> x2, blocking collectives: 76.3 us -> 31.8 us  [exchange(): return lax.all_to_all(value, axes, 0, 0, tiled=True)]
    all_to_all x1 -> x2, starting transfers between devices: 5.67 us -> 27.5 us  [exchange(): return lax.all_to_all(value, axes, 0, 0, tiled=True)]
    all_gather x0 -> x4, blocking collectives: none -> 20 us  [gathered(): value = lax.all_gather(value, axes, tiled=True)]
    all_to_all x1 -> x2, waiting for transfers between devices: 2.7 us -> 2.97 us  [exchange(): return lax.all_to_all(value, axes, 0, 0, tiled=True)]
  transfers between devices with their start and end apart: 1 -> 2, of which waited for: 1 -> 1; matrix products, arithmetic and copies ran while one was open for 0% -> 0% of each run, Pallas kernels for 9% -> 8%
where the time goes in v3:
time: 101 us
  blocking collectives  51.8 us (51%)
  starting transfers between devices  27.5 us (27%)
  Pallas kernels  17.9 us (18%)
  waiting for transfers between devices  2.97 us (3%)
    all_to_all x2, blocking collectives, exchange(): return lax.all_to_all(value, axes, 0, 0, tiled=True)  31.8 us
    all_to_all x2, starting transfers between devices, exchange(): return lax.all_to_all(value, axes, 0, 0, tiled=True)  27.5 us
    all_gather x4, blocking collectives, gathered(): value = lax.all_gather(value, axes, tiled=True)  20 us
    pallas_call x6, Pallas kernels, call(): pl.pallas_call(kernel, out_shape=[jax.ShapeDtypeStruct(s, F32) for s in o...  17.9 us
    all_to_all x2, waiting for transfers between devices, exchange(): return lax.all_to_all(value, axes, 0, 0, tiled=True)  2.97 us
  transfers between devices with their start and end apart: 2, of which 1 were waited for; matrix products, arithmetic and copies ran while one was open for 0% of the time, Pallas kernels for 8%

profile of v3, /device:TPU:1, one launch (start us, length us, event | category | flops | bytes accessed | tf_op | source)
XLA Modules:
  0.0 101.0 jit_solution(11599335957983677205)
XLA Ops:
  0.6 2.2 %shard_map.119 = (f32[16,16,256]{2,1,0:T(8,128)}, f32[8,128]{1,0:T(8,128)}, f32[256,128]{1,0:T(8,128)}, f32[2,128,24]{2,1,0:T(8,128)}, f32[16,256]{1,0:T(8,128)}) custom-call(f32[3,256]{1,0:T(4,128)} %refs_0_.1, f32[3,256]{1,0:T(4,128)} %refs_1_.1, f32[3,256]{1,0:T(4,128)} %refs_2_.1, f32[3,256]{1,0:T(4,128)} %refs_3_.1, f32[1,256]{1,0:T(1,128)} %bitcast.6, ...), custom_call_target="tpu_custom_call" | custom-call | tf_op jit(solution)/shard_map/pallas_call | solution.py:316
  2.9 0.0 copy-start.3
  2.9 15.8 %all-to-all-start = ((f32[16,16,256]{2,1,0:T(8,128)}), f32[16,16,256]{2,1,0:T(8,128)S(1)}, u32[]{:S(2)}, u32[]{:S(2)}) async-start(f32[16,16,256]{2,1,0:T(8,128)} %get-tuple-element.22), calls=%async_computation | async-start | bytes 524288 | tf_op jit(solution)/shard_map/all_to_all | solution.py:337
  18.6 0.0 copy-done.3
  18.7 5.9 %all_gather.12 = f32[32,128]{1,0:T(8,128)S(1)} all-gather(f32[8,128]{1,0:T(8,128)S(1)} %copy-done.3), channel_id=1, replica_groups=mesh['a'=2,'b'=2,'h'=2,'z'=16,'l'=2,'c'=2] {'l','c'}, dimensions={0}, use_global_device_ids=true | all-gather | bytes 20480 | tf_op jit(solution)/shard_map/all_gather | solution.py:332
  24.6 5.1 %all_gather.13 = f32[64,128]{1,0:T(8,128)S(1)} all-gather(f32[32,128]{1,0:T(8,128)S(1)} %all_gather.12), channel_id=1, replica_groups=mesh['a'=2,'b'=2,'h'=2,'z'=16,'l'=2,'c'=2] {'h'}, dimensions={0}, use_global_device_ids=true | all-gather | bytes 49152 | tf_op jit(solution)/shard_map/all_gather | solution.py:332
  29.6 3.7 %all_gather.14 = f32[128,128]{1,0:T(8,128)S(1)} all-gather(f32[64,128]{1,0:T(8,128)S(1)} %all_gather.13), channel_id=1, replica_groups=mesh['a'=2,'b'=2,'h'=2,'z'=16,'l'=2,'c'=2] {'b'}, dimensions={0}, use_global_device_ids=true | all-gather | bytes 98304 | tf_op jit(solution)/shard_map/all_gather | solution.py:332
  33.4 5.3 %all_gather.15 = f32[256,128]{1,0:T(8,128)S(1)} all-gather(f32[128,128]{1,0:T(8,128)S(1)} %all_gather.14), channel_id=1, replica_groups=mesh['a'=2,'b'=2,'h'=2,'z'=16,'l'=2,'c'=2] {'a'}, dimensions={0}, use_global_device_ids=true | all-gather | bytes 196608 | tf_op jit(solution)/shard_map/all_gather | solution.py:332
  38.7 0.0 all-to-all-done.zrecv
  38.7 4.3 %shard_map.120 = (f32[32,2,1152]{2,1,0:T(2,128)S(1)}, f32[16,384]{1,0:T(8,128)S(1)}, f32[8,384]{1,0:T(8,128)S(1)}) custom-call(f32[16,16,256]{2,1,0:T(8,128)S(1)} %all-to-all-done.zrecv, f32[32,8,128]{2,1,0:T(8,128)S(1)} %bitcast.5), custom_call_target="tpu_custom_call" | custom-call | tf_op jit(solution)/shard_map/pallas_call | solution.py:316
  43.0 19.2 %all_to_all.20.precv = f32[32,2,1152]{2,1,0:T(2,128)S(1)} all-to-all(f32[32,2,1152]{2,1,0:T(2,128)S(1)} %get-tuple-element.24), channel_id=1, replica_groups=mesh['a'=2,'b'=2,'h'=2,'z'=16,'l'=2,'c'=2] {'a','b','h','l','c'}, dimensions={0} | all-to-all | bytes 589824 | tf_op jit(solution)/shard_map/all_to_all | solution.py:337
  62.2 0.9 shard_map.121
  63.1 11.7 %all-to-all-start.2 = ((f32[16,1,128]{2,1,0:T(1,128)}), f32[16,1,128]{2,1,0:T(1,128)S(1)}, u32[]{:S(2)}, u32[]{:S(2)}) async-start(f32[16,1,128]{2,1,0:T(1,128)} %get-tuple-element.26), calls=%async_computation.2 | async-start | bytes 16384 | tf_op jit(solution)/shard_map/all_to_all | solution.py:337
  74.8 8.3 %shard_map.122.part = f32[8,768]{1,0:T(8,128)S(1)} custom-call(f32[16,16,256]{2,1,0:T(8,128)S(1)} %all-to-all-done.zrecv, f32[8,384]{1,0:T(8,128)S(1)} %get-tuple-element.27.moved, f32[8,384]{1,0:T(8,128)S(1)} %get-tuple-element.28.other), custom_call_target="tpu_custom_call" | custom-call | tf_op jit(solution)/shard_map/pallas_call | solution.py:316
  83.2 3.0 %all-to-all-done.2.zrecv = f32[16,1,128]{2,1,0:T(1,128)S(1)} async-done(((f32[16,1,128]{2,1,0:T(1,128)}), f32[16,1,128]{2,1,0:T(1,128)S(1)}, u32[]{:S(2)}, u32[]{:S(2)}) %all-to-all-start.2) | async-done | bytes 8224 | tf_op jit(solution)/shard_map/all_to_all | solution.py:337
  86.1 0.0 copy-start.2
  86.1 1.1 %shard_map.123 = f32[32,8,128]{2,1,0:T(8,128)S(1)} custom-call(f32[16,1,128]{2,1,0:T(1,128)S(1)} %all-to-all-done.2.zrecv, f32[8,384]{1,0:T(8,128)S(1)} %get-tuple-element.27.moved, f32[8,384]{1,0:T(8,128)S(1)} %get-tuple-element.28.other, f32[8,768]{1,0:T(8,128)S(1)} %shard_map.122.part), custom_call_target="tpu_custom_call" | custom-call | tf_op jit(solution)/shard_map/pallas_call | solution.py:316
  87.2 0.0 copy-start
  87.2 0.0 copy-start.1
  87.2 12.7 %all_to_all.21.frecv = f32[32,8,128]{2,1,0:T(8,128)S(1)} all-to-all(f32[32,8,128]{2,1,0:T(8,128)S(1)} %shard_map.123), channel_id=1, replica_groups=mesh['a'=2,'b'=2,'h'=2,'z'=16,'l'=2,'c'=2] {'a','b','h','l','c'}, dimensions={0} | all-to-all | bytes 262144 | tf_op jit(solution)/shard_map/all_to_all | solution.py:337
  99.9 0.0 copy-done.2
  99.9 0.0 copy-done
  99.9 0.0 copy-done.1
  99.9 1.1 %shard_map.124 = (f32[3,256]{1,0:T(4,128)}, f32[3,256]{1,0:T(4,128)}, f32[3,256]{1,0:T(4,128)}, f32[3,256]{1,0:T(4,128)}, f32[6,2,24]{2,1,0:T(2,128)}) custom-call(f32[16,256]{1,0:T(8,128)S(1)} %copy-done.2, f32[32,8,128]{2,1,0:T(8,128)S(1)} %all_to_all.21.frecv, f32[8,128]{1,0:T(8,128)S(1)} %get-tuple-element.29.mine, f32[256,128]{1,0:T(8,128)S(1)} %copy-done, ...), custom_call_target="tpu_custom_call" | custom-call | tf_op jit(solution)/shard_map/pallas_call | solution.py:316
Async XLA Ops:
  2.9 15.8 %copy-start.3 = (f32[8,128]{1,0:T(8,128)S(1)}, f32[8,128]{1,0:T(8,128)}, u32[]{:S(2)}) copy-start(f32[8,128]{1,0:T(8,128)} %get-tuple-element.23) | copy-start | bytes 12292
  2.9 35.8 %all-to-all-start = ((f32[16,16,256]{2,1,0:T(8,128)}), f32[16,16,256]{2,1,0:T(8,128)S(1)}, u32[]{:S(2)}, u32[]{:S(2)}) async-start(f32[16,16,256]{2,1,0:T(8,128)} %get-tuple-element.22), calls=%async_computation | async-start | bytes 524288 | tf_op jit(solution)/shard_map/all_to_all | solution.py:337
  63.1 23.0 %all-to-all-start.2 = ((f32[16,1,128]{2,1,0:T(1,128)}), f32[16,1,128]{2,1,0:T(1,128)S(1)}, u32[]{:S(2)}, u32[]{:S(2)}) async-start(f32[16,1,128]{2,1,0:T(1,128)} %get-tuple-element.26), calls=%async_computation.2 | async-start | bytes 16384 | tf_op jit(solution)/shard_map/all_to_all | solution.py:337
  86.1 13.8 %copy-start.2 = (f32[16,256]{1,0:T(8,128)S(1)}, f32[16,256]{1,0:T(8,128)}, u32[]{:S(2)}) copy-start(f32[16,256]{1,0:T(8,128)} %get-tuple-element.21.keep) | copy-start | bytes 49156
  87.2 12.7 %copy-start = (f32[256,128]{1,0:T(8,128)S(1)}, f32[256,128]{1,0:T(8,128)}, u32[]{:S(2)}) copy-start(f32[256,128]{1,0:T(8,128)} %get-tuple-element.30.place) | copy-start | bytes 393220
  87.2 12.7 %copy-start.1 = (f32[2,128,24]{2,1,0:T(8,128)S(1)}, f32[2,128,24]{2,1,0:T(8,128)}, u32[]{:S(2)}) copy-start(f32[2,128,24]{2,1,0:T(8,128)} %get-tuple-element.31.slots) | copy-start | bytes 73732

commit v4 on v3

--- a/solution.py
+++ b/solution.py
@@ -141,8 +141,14 @@
     return high, middle, value - high - middle
 
 
-def source_parts(rows, feats, values):
+def middle_of(states):
+    mean = jnp.sum(states, axis=1, keepdims=True) / states.shape[1]
+    return jnp.where(iota(mean.shape, 0) < 6, mean, 0.0)
+
+
+def source_parts(rows, middle, feats, values):
     count = rows.shape[0]
+    rows = rows - jnp.concatenate([middle] * (count // 8), axis=0)
     row = iota(rows.shape, 0) % 8
 
     def ahead(value, by):
@@ -215,10 +221,11 @@
         known[0:8, here] = block[:, 0:SLOTS]
         known[8:16, here] = block[:, RATES : RATES + SLOTS]
         other[:, here] = block[:, LISTED : LISTED + SLOTS]
-    source_parts(zrecv[:, 0:8, :].reshape(8 * COLUMN, PART), feats, values)
     p1, v1 = predict(known[0:3], known[3:6], known[8:11], known[11:14], STEP_BASE)
     states = jnp.concatenate([p1, v1, jnp.zeros((2, COLS), F32)], axis=0)
-    part = pair_sums(states, feats, values, 8 * PART)
+    middle = middle_of(states)
+    source_parts(zrecv[:, 0:8, :].reshape(8 * COLUMN, PART), middle, feats, values)
+    part = pair_sums(states - middle, feats, values, 8 * PART)
     halves = [jnp.concatenate([part[3 * row + k : 3 * row + k + 1] for k in range(3)], axis=1) for row in range(2)]
     both = jnp.concatenate(halves, axis=0)
     for k in range(PLANE):
@@ -226,9 +233,10 @@
 
 
 def later_kernel(zrecv, moved, other, out, feats, values):
-    source_parts(zrecv[:, 8:16, :].reshape(8 * COLUMN, PART), feats, values)
-    out[:, 0:COLS] = pair_sums(moved[...], feats, values, 8 * PART)
-    out[:, COLS:] = pair_sums(other[...], feats, values, 8 * PART)
+    middle = middle_of(moved[...])
+    source_parts(zrecv[:, 8:16, :].reshape(8 * COLUMN, PART), middle, feats, values)
+    out[:, 0:COLS] = pair_sums(moved[...] - middle, feats, values, 8 * PART)
+    out[:, COLS:] = pair_sums(other[...] - middle, feats, values, 8 * PART)
 
 
 def update_kernel(precv, known, zsend, moved, mine):
@@ -271,8 +279,9 @@
             item = jnp.where(lane < 16, pltpu.roll(packed, (LANES - 16 * k) % LANES, 1), 0.0)
             item = pltpu.roll(item, 0, 1, stride=16, stride_axis=0)
             rows[k : k + 1, LANES * half : LANES * (half + 1)] = jnp.sum(item, axis=0, keepdims=True)
-    source_parts(rows[...], feats, values)
-    states = jnp.concatenate([moved[...], other[...]], axis=1)
+    middle = middle_of(moved[...])
+    source_parts(rows[...], middle, feats, values)
+    states = jnp.concatenate([moved[...], other[...]], axis=1) - middle
     sums[...] = pair_sums(states, feats, values, PART) + part[...]
     for q in range(CHIPS):
         here = slice(SLOTS * q, SLOTS * (q + 1))

time: 101 us -> 102 us (level)
  no operation moved by 1% of the time
where the time goes in v4:
time: 102 us; the launch traced here: 101 us
  blocking collectives  51.8 us (51%)
  starting transfers between devices  27.5 us (27%)
  Pallas kernels  18.2 us (18%)
  waiting for transfers between devices  2.87 us (3%)
    all_to_all x2, blocking collectives, exchange(): return lax.all_to_all(value, axes, 0, 0, tiled=True)  31.8 us
    all_to_all x2, starting transfers between devices, exchange(): return lax.all_to_all(value, axes, 0, 0, tiled=True)  27.5 us
    all_gather x4, blocking collectives, gathered(): value = lax.all_gather(value, axes, tiled=True)  20 us
    pallas_call x6, Pallas kernels, call(): pl.pallas_call(kernel, out_shape=[jax.ShapeDtypeStruct(s, F32) for s in o...  18.2 us
    all_to_all x2, waiting for transfers between devices, exchange(): return lax.all_to_all(value, axes, 0, 0, tiled=True)  2.87 us
  transfers between devices with their start and end apart: 2, of which 1 were waited for; matrix products, arithmetic and copies ran while one was open for 0% of the time, Pallas kernels for 8%

profile of v4, /device:TPU:1, one launch (start us, length us, event | category | flops | bytes accessed | tf_op | source)
XLA Modules:
  0.0 101.1 jit_solution(11600774424881916079)
XLA Ops:
  0.6 2.2 %shard_map.119 = (f32[16,16,256]{2,1,0:T(8,128)}, f32[8,128]{1,0:T(8,128)}, f32[256,128]{1,0:T(8,128)}, f32[2,128,24]{2,1,0:T(8,128)}, f32[16,256]{1,0:T(8,128)}) custom-call(f32[3,256]{1,0:T(4,128)} %refs_0_.1, f32[3,256]{1,0:T(4,128)} %refs_1_.1, f32[3,256]{1,0:T(4,128)} %refs_2_.1, f32[3,256]{1,0:T(4,128)} %refs_3_.1, f32[1,256]{1,0:T(1,128)} %bitcast.6, ...), custom_call_target="tpu_custom_call" | custom-call | tf_op jit(solution)/shard_map/pallas_call | solution.py:325
  2.9 0.0 copy-start.3
  2.9 15.8 %all-to-all-start = ((f32[16,16,256]{2,1,0:T(8,128)}), f32[16,16,256]{2,1,0:T(8,128)S(1)}, u32[]{:S(2)}, u32[]{:S(2)}) async-start(f32[16,16,256]{2,1,0:T(8,128)} %get-tuple-element.22), calls=%async_computation | async-start | bytes 524288 | tf_op jit(solution)/shard_map/all_to_all | solution.py:346
  18.6 0.0 copy-done.3
  18.7 5.9 %all_gather.12 = f32[32,128]{1,0:T(8,128)S(1)} all-gather(f32[8,128]{1,0:T(8,128)S(1)} %copy-done.3), channel_id=1, replica_groups=mesh['a'=2,'b'=2,'h'=2,'z'=16,'l'=2,'c'=2] {'l','c'}, dimensions={0}, use_global_device_ids=true | all-gather | bytes 20480 | tf_op jit(solution)/shard_map/all_gather | solution.py:341
  24.6 5.1 %all_gather.13 = f32[64,128]{1,0:T(8,128)S(1)} all-gather(f32[32,128]{1,0:T(8,128)S(1)} %all_gather.12), channel_id=1, replica_groups=mesh['a'=2,'b'=2,'h'=2,'z'=16,'l'=2,'c'=2] {'h'}, dimensions={0}, use_global_device_ids=true | all-gather | bytes 49152 | tf_op jit(solution)/shard_map/all_gather | solution.py:341
  29.6 3.7 %all_gather.14 = f32[128,128]{1,0:T(8,128)S(1)} all-gather(f32[64,128]{1,0:T(8,128)S(1)} %all_gather.13), channel_id=1, replica_groups=mesh['a'=2,'b'=2,'h'=2,'z'=16,'l'=2,'c'=2] {'b'}, dimensions={0}, use_global_device_ids=true | all-gather | bytes 98304 | tf_op jit(solution)/shard_map/all_gather | solution.py:341
  33.4 5.3 %all_gather.15 = f32[256,128]{1,0:T(8,128)S(1)} all-gather(f32[128,128]{1,0:T(8,128)S(1)} %all_gather.14), channel_id=1, replica_groups=mesh['a'=2,'b'=2,'h'=2,'z'=16,'l'=2,'c'=2] {'a'}, dimensions={0}, use_global_device_ids=true | all-gather | bytes 196608 | tf_op jit(solution)/shard_map/all_gather | solution.py:341
  38.7 0.0 all-to-all-done.zrecv
  38.7 4.5 %shard_map.120 = (f32[32,2,1152]{2,1,0:T(2,128)S(1)}, f32[16,384]{1,0:T(8,128)S(1)}, f32[8,384]{1,0:T(8,128)S(1)}) custom-call(f32[16,16,256]{2,1,0:T(8,128)S(1)} %all-to-all-done.zrecv, f32[32,8,128]{2,1,0:T(8,128)S(1)} %bitcast.5), custom_call_target="tpu_custom_call" | custom-call | tf_op jit(solution)/shard_map/pallas_call | solution.py:325
  43.1 19.2 %all_to_all.20.precv = f32[32,2,1152]{2,1,0:T(2,128)S(1)} all-to-all(f32[32,2,1152]{2,1,0:T(2,128)S(1)} %get-tuple-element.24), channel_id=1, replica_groups=mesh['a'=2,'b'=2,'h'=2,'z'=16,'l'=2,'c'=2] {'a','b','h','l','c'}, dimensions={0} | all-to-all | bytes 589824 | tf_op jit(solution)/shard_map/all_to_all | solution.py:346
  62.3 0.9 shard_map.121
  63.2 11.7 %all-to-all-start.2 = ((f32[16,1,128]{2,1,0:T(1,128)}), f32[16,1,128]{2,1,0:T(1,128)S(1)}, u32[]{:S(2)}, u32[]{:S(2)}) async-start(f32[16,1,128]{2,1,0:T(1,128)} %get-tuple-element.26), calls=%async_computation.2 | async-start | bytes 16384 | tf_op jit(solution)/shard_map/all_to_all | solution.py:346
  75.0 8.4 %shard_map.122.part = f32[8,768]{1,0:T(8,128)S(1)} custom-call(f32[16,16,256]{2,1,0:T(8,128)S(1)} %all-to-all-done.zrecv, f32[8,384]{1,0:T(8,128)S(1)} %get-tuple-element.27.moved, f32[8,384]{1,0:T(8,128)S(1)} %get-tuple-element.28.other), custom_call_target="tpu_custom_call" | custom-call | tf_op jit(solution)/shard_map/pallas_call | solution.py:325
  83.4 2.9 %all-to-all-done.2.zrecv = f32[16,1,128]{2,1,0:T(1,128)S(1)} async-done(((f32[16,1,128]{2,1,0:T(1,128)}), f32[16,1,128]{2,1,0:T(1,128)S(1)}, u32[]{:S(2)}, u32[]{:S(2)}) %all-to-all-start.2) | async-done | bytes 8224 | tf_op jit(solution)/shard_map/all_to_all | solution.py:346
  86.3 0.0 copy-start.2
  86.3 1.1 %shard_map.123 = f32[32,8,128]{2,1,0:T(8,128)S(1)} custom-call(f32[16,1,128]{2,1,0:T(1,128)S(1)} %all-to-all-done.2.zrecv, f32[8,384]{1,0:T(8,128)S(1)} %get-tuple-element.27.moved, f32[8,384]{1,0:T(8,128)S(1)} %get-tuple-element.28.other, f32[8,768]{1,0:T(8,128)S(1)} %shard_map.122.part), custom_call_target="tpu_custom_call" | custom-call | tf_op jit(solution)/shard_map/pallas_call | solution.py:325
  87.4 0.0 copy-start
  87.4 0.0 copy-start.1
  87.4 12.7 %all_to_all.21.frecv = f32[32,8,128]{2,1,0:T(8,128)S(1)} all-to-all(f32[32,8,128]{2,1,0:T(8,128)S(1)} %shard_map.123), channel_id=1, replica_groups=mesh['a'=2,'b'=2,'h'=2,'z'=16,'l'=2,'c'=2] {'a','b','h','l','c'}, dimensions={0} | all-to-all | bytes 262144 | tf_op jit(solution)/shard_map/all_to_all | solution.py:346
  100.1 0.0 copy-done.2
  100.1 0.0 copy-done
  100.1 0.0 copy-done.1
  100.1 1.1 %shard_map.124 = (f32[3,256]{1,0:T(4,128)}, f32[3,256]{1,0:T(4,128)}, f32[3,256]{1,0:T(4,128)}, f32[3,256]{1,0:T(4,128)}, f32[6,2,24]{2,1,0:T(2,128)}) custom-call(f32[16,256]{1,0:T(8,128)S(1)} %copy-done.2, f32[32,8,128]{2,1,0:T(8,128)S(1)} %all_to_all.21.frecv, f32[8,128]{1,0:T(8,128)S(1)} %get-tuple-element.29.mine, f32[256,128]{1,0:T(8,128)S(1)} %copy-done, ...), custom_call_target="tpu_custom_call" | custom-call | tf_op jit(solution)/shard_map/pallas_call | solution.py:325
Async XLA Ops:
  2.9 15.8 %copy-start.3 = (f32[8,128]{1,0:T(8,128)S(1)}, f32[8,128]{1,0:T(8,128)}, u32[]{:S(2)}) copy-start(f32[8,128]{1,0:T(8,128)} %get-tuple-element.23) | copy-start | bytes 12292
  2.9 35.8 %all-to-all-start = ((f32[16,16,256]{2,1,0:T(8,128)}), f32[16,16,256]{2,1,0:T(8,128)S(1)}, u32[]{:S(2)}, u32[]{:S(2)}) async-start(f32[16,16,256]{2,1,0:T(8,128)} %get-tuple-element.22), calls=%async_computation | async-start | bytes 524288 | tf_op jit(solution)/shard_map/all_to_all | solution.py:346
  63.2 23.0 %all-to-all-start.2 = ((f32[16,1,128]{2,1,0:T(1,128)}), f32[16,1,128]{2,1,0:T(1,128)S(1)}, u32[]{:S(2)}, u32[]{:S(2)}) async-start(f32[16,1,128]{2,1,0:T(1,128)} %get-tuple-element.26), calls=%async_computation.2 | async-start | bytes 16384 | tf_op jit(solution)/shard_map/all_to_all | solution.py:346
  86.3 13.8 %copy-start.2 = (f32[16,256]{1,0:T(8,128)S(1)}, f32[16,256]{1,0:T(8,128)}, u32[]{:S(2)}) copy-start(f32[16,256]{1,0:T(8,128)} %get-tuple-element.21.keep) | copy-start | bytes 49156
  87.4 12.7 %copy-start = (f32[256,128]{1,0:T(8,128)S(1)}, f32[256,128]{1,0:T(8,128)}, u32[]{:S(2)}) copy-start(f32[256,128]{1,0:T(8,128)} %get-tuple-element.30.place) | copy-start | bytes 393220
  87.4 12.7 %copy-start.1 = (f32[2,128,24]{2,1,0:T(8,128)S(1)}, f32[2,128,24]{2,1,0:T(8,128)}, u32[]{:S(2)}) copy-start(f32[2,128,24]{2,1,0:T(8,128)} %get-tuple-element.31.slots) | copy-start | bytes 73732

commit v5 on v4

--- a/solution.py
+++ b/solution.py
@@ -19,7 +19,6 @@
 RATES = 64
 ALL_AXES = ("a", "b", "h", "z", "l", "c")
 PLANE_AXES = ("a", "b", "h", "l", "c")
-STAGES = (("l", "c"), "h", "b", "a")
 EXACT = lax.Precision.HIGHEST
 F32 = jnp.float32
 I32 = jnp.int32
@@ -48,7 +47,7 @@
 
 def prepare_kernel(
     total, pos_h, vel_h, acc_h, jerk_h, weight_h, lev_h, active_h, counts_h, zsend, isend, place, slots, keep,
-    jrows, srows, state, weight, levels, active, counts, sems,
+    srows, state, weight, levels, active, counts, sems,
 ):
     copies = [
         pltpu.make_async_copy(src, dst, sems.at[k])
@@ -79,17 +78,14 @@
         keep[3 * k : 3 * k + 3] = part
     keep[12:13] = lev.astype(F32)
     keep[13:16] = jnp.zeros((3, PART), F32)
-    jrows[0:3] = p1
-    jrows[3:6] = v1
-    jrows[6:7] = mass
-    jrows[7:8] = jnp.zeros((1, PART), F32)
-    jrows[8:11] = p2
-    jrows[11:14] = v2
-    jrows[14:15] = jnp.where(lev == 0, 0.0, mass)
-    jrows[15:16] = jnp.zeros((1, PART), F32)
-    rows = jrows[...]
+    later_mass = jnp.where(lev == 0, 0.0, mass)
+    lines = [
+        jnp.concatenate([part[k : k + 1] for part in (x, w) for k in range(3)] + [m], axis=1)
+        for x, w, m in ((p1, v1, mass), (p2, v2, later_mass))
+    ]
+    both = jnp.concatenate(lines, axis=0)
     for k in range(COLUMN):
-        zsend[k] = rows
+        zsend[k] = both
     srows[...] = jnp.zeros(srows.shape, F32)
     srows[0:3] = p
     srows[3:6] = v
@@ -128,7 +124,8 @@
     picked = jnp.dot(srows[...], spots, precision=EXACT, preferred_element_type=F32)
     lane = iota((8, LANES), 1)
     payload = jnp.where(lane < LISTED, picked[0:8], jnp.where(lane < RATES, picked[8:16], picked[16:24]))
-    isend[...] = payload
+    for k in range(PLANE):
+        isend[k] = payload
 
 
 def rounded(value):
@@ -214,7 +211,16 @@
     return jnp.concatenate([acc, jerk, jnp.zeros((2, states.shape[1]), F32)], axis=0)
 
 
-def first_kernel(zrecv, irecv, psend, known, other, feats, values):
+def unpacked(zrecv, step, rows):
+    rows[...] = jnp.zeros(rows.shape, F32)
+    for k in range(7):
+        for half in range(2):
+            start = PART * k + LANES * half
+            rows[half, pl.ds(k, COLUMN, stride=8), :] = zrecv[:, step, start : start + LANES]
+    return jnp.concatenate([rows[0], rows[1]], axis=1)
+
+
+def first_kernel(zrecv, irecv, psend, known, other, feats, values, rows):
     for q in range(CHIPS):
         block = irecv[2 * q] + irecv[2 * q + 1]
         here = slice(SLOTS * q, SLOTS * (q + 1))
@@ -224,7 +230,7 @@
     p1, v1 = predict(known[0:3], known[3:6], known[8:11], known[11:14], STEP_BASE)
     states = jnp.concatenate([p1, v1, jnp.zeros((2, COLS), F32)], axis=0)
     middle = middle_of(states)
-    source_parts(zrecv[:, 0:8, :].reshape(8 * COLUMN, PART), middle, feats, values)
+    source_parts(unpacked(zrecv, 0, rows), middle, feats, values)
     part = pair_sums(states - middle, feats, values, 8 * PART)
     halves = [jnp.concatenate([part[3 * row + k : 3 * row + k + 1] for k in range(3)], axis=1) for row in range(2)]
     both = jnp.concatenate(halves, axis=0)
@@ -232,9 +238,9 @@
         psend[k] = both
 
 
-def later_kernel(zrecv, moved, other, out, feats, values):
+def later_kernel(zrecv, moved, other, out, feats, values, rows):
     middle = middle_of(moved[...])
-    source_parts(zrecv[:, 8:16, :].reshape(8 * COLUMN, PART), middle, feats, values)
+    source_parts(unpacked(zrecv, 1, rows), middle, feats, values)
     out[:, 0:COLS] = pair_sums(moved[...] - middle, feats, values, 8 * PART)
     out[:, COLS:] = pair_sums(other[...] - middle, feats, values, 8 * PART)
 
@@ -336,10 +342,8 @@
     return [pltpu.VMEM((64, sources), BF16), pltpu.VMEM((32, sources), BF16)]
 
 
-def gathered(value):
-    for axes in STAGES:
-        value = lax.all_gather(value, axes, tiled=True)
-    return value.reshape(PLANE, 8, LANES)
+def sources_scratch():
+    return operands(COLUMN * PART) + [pltpu.VMEM((2, 8 * COLUMN, LANES), F32)]
 
 
 def exchange(value, axes):
@@ -357,9 +361,8 @@
     zsend, isend, place, slots, keep = call(
         prepare,
         (*state, mass_weight.reshape(1, PART), lev, active, counts.reshape(1, 2)),
-        [(COLUMN, 16, PART), (8, LANES), (PART, LANES), (2, LANES, SLOTS), (16, PART)],
+        [(COLUMN, 2, 7 * PART), (PLANE, 8, LANES), (PART, LANES), (2, LANES, SLOTS), (16, PART)],
         [
-            pltpu.VMEM((16, PART), F32),
             pltpu.VMEM((24, PART), F32),
             pltpu.VMEM((4, 3, PART), F32),
             pltpu.VMEM((1, PART), F32),
@@ -371,15 +374,15 @@
         far=8,
         mib=60,
     )
-    irecv = gathered(isend)
+    irecv = exchange(isend, PLANE_AXES)
     zrecv = exchange(zsend, "z")
     psend, known, other = call(
-        first_kernel, (zrecv, irecv), [(PLANE, 2, 3 * COLS), (16, COLS), (8, COLS)], operands(COLUMN * PART), mib=24
+        first_kernel, (zrecv, irecv), [(PLANE, 2, 3 * COLS), (16, COLS), (8, COLS)], sources_scratch(), mib=24
     )
     precv = exchange(psend, PLANE_AXES)
     zsend2, moved, mine = call(update_kernel, (precv, known), [(COLUMN, 1, LANES), (8, COLS), (8, LANES)])
     zrecv2 = exchange(zsend2, "z")
-    (part,) = call(later_kernel, (zrecv, moved, other), [(8, 2 * COLS)], operands(COLUMN * PART), mib=24)
+    (part,) = call(later_kernel, (zrecv, moved, other), [(8, 2 * COLS)], sources_scratch(), mib=24)
     (fsend,) = call(
         last_kernel,
         (zrecv2, moved, other, part),

time: 102 us -> 102 us (level)
  blocking collectives: 51.8 us -> 74 us
  starting transfers between devices: 27.5 us -> 5.6 us
    all_to_all x2 -> x4, blocking collectives: 31.8 us -> 74 us  [exchange(): return lax.all_to_all(value, axes, 0, 0, tiled=True)]
    all_to_all x2 -> x1, starting transfers between devices: 27.5 us -> 5.6 us  [exchange(): return lax.all_to_all(value, axes, 0, 0, tiled=True)]
    all_gather x4 -> x0, blocking collectives: 20 us -> none  [gathered(): value = lax.all_gather(value, axes, tiled=True)]
    all_to_all x2 -> x1, waiting for transfers between devices: 2.87 us -> 2.81 us  [exchange(): return lax.all_to_all(value, axes, 0, 0, tiled=True)]
  transfers between devices with their start and end apart: 2 -> 1, of which waited for: 1 -> 1; matrix products, arithmetic and copies ran while one was open for 0% -> 0% of each run, Pallas kernels for 8% -> 8%
where the time goes in v5:
time: 102 us; the launch traced here: 101 us
  blocking collectives  74 us (73%)
  Pallas kernels  18.3 us (18%)
  starting transfers between devices  5.6 us (5%)
  waiting for transfers between devices  2.81 us (3%)
    all_to_all x4, blocking collectives, exchange(): return lax.all_to_all(value, axes, 0, 0, tiled=True)  74 us
    pallas_call x6, Pallas kernels, call(): pl.pallas_call(kernel, out_shape=[jax.ShapeDtypeStruct(s, F32) for s in o...  18.3 us
    all_to_all x1, starting transfers between devices, exchange(): return lax.all_to_all(value, axes, 0, 0, tiled=True)  5.6 us
    all_to_all x1, waiting for transfers between devices, exchange(): return lax.all_to_all(value, axes, 0, 0, tiled=True)  2.81 us
  transfers between devices with their start and end apart: 1, of which 1 were waited for; matrix products, arithmetic and copies ran while one was open for 0% of the time, Pallas kernels for 8%

profile of v5, /device:TPU:1, one launch (start us, length us, event | category | flops | bytes accessed | tf_op | source)
XLA Modules:
  0.0 101.4 jit_solution(10117438666341012630)
XLA Ops:
  0.6 2.3 %shard_map.119 = (f32[16,2,1792]{2,1,0:T(2,128)}, f32[32,8,128]{2,1,0:T(8,128)}, f32[256,128]{1,0:T(8,128)}, f32[2,128,24]{2,1,0:T(8,128)}, f32[16,256]{1,0:T(8,128)}) custom-call(f32[3,256]{1,0:T(4,128)} %refs_0_.1, f32[3,256]{1,0:T(4,128)} %refs_1_.1, f32[3,256]{1,0:T(4,128)} %refs_2_.1, f32[3,256]{1,0:T(4,128)} %refs_3_.1, f32[1,256]{1,0:T(1,128)} %bitcast.4, ...), custom_call_target="tpu_custom_call" | custom-call | tf_op jit(solution)/shard_map/pallas_call | solution.py:331
  2.9 0.0 copy-start.3
  2.9 18.2 %all_to_all.25.irecv = f32[32,8,128]{2,1,0:T(8,128)S(1)} all-to-all(f32[32,8,128]{2,1,0:T(8,128)} %get-tuple-element.23), channel_id=1, replica_groups=mesh['a'=2,'b'=2,'h'=2,'z'=16,'l'=2,'c'=2] {'a','b','h','l','c'}, dimensions={0} | all-to-all | bytes 262144 | tf_op jit(solution)/shard_map/all_to_all | solution.py:350
  21.2 0.0 copy-done.3
  21.2 26.2 %all_to_all.26.zrecv = f32[16,2,1792]{2,1,0:T(2,128)S(1)} all-to-all(f32[16,2,1792]{2,1,0:T(2,128)S(1)} %copy-done.3), channel_id=1, replica_groups=mesh['a'=2,'b'=2,'h'=2,'z'=16,'l'=2,'c'=2] {'z'}, dimensions={0} | all-to-all | bytes 458752 | tf_op jit(solution)/shard_map/all_to_all | solution.py:350
  47.3 4.5 %shard_map.120 = (f32[32,2,1152]{2,1,0:T(2,128)S(1)}, f32[16,384]{1,0:T(8,128)S(1)}, f32[8,384]{1,0:T(8,128)S(1)}) custom-call(f32[16,2,1792]{2,1,0:T(2,128)S(1)} %all_to_all.26.zrecv, f32[32,8,128]{2,1,0:T(8,128)S(1)} %all_to_all.25.irecv), custom_call_target="tpu_custom_call" | custom-call | tf_op jit(solution)/shard_map/pallas_call | solution.py:331
  51.9 16.8 %all_to_all.27.precv = f32[32,2,1152]{2,1,0:T(2,128)S(1)} all-to-all(f32[32,2,1152]{2,1,0:T(2,128)S(1)} %get-tuple-element.24), channel_id=1, replica_groups=mesh['a'=2,'b'=2,'h'=2,'z'=16,'l'=2,'c'=2] {'a','b','h','l','c'}, dimensions={0} | all-to-all | bytes 589824 | tf_op jit(solution)/shard_map/all_to_all | solution.py:350
  68.7 0.9 shard_map.121
  69.6 5.6 %all-to-all-start.3 = ((f32[16,1,128]{2,1,0:T(1,128)}), f32[16,1,128]{2,1,0:T(1,128)S(1)}, u32[]{:S(2)}, u32[]{:S(2)}) async-start(f32[16,1,128]{2,1,0:T(1,128)} %get-tuple-element.26), calls=%async_computation.3 | async-start | bytes 16384 | tf_op jit(solution)/shard_map/all_to_all | solution.py:350
  75.2 8.4 %shard_map.122.part = f32[8,768]{1,0:T(8,128)S(1)} custom-call(f32[16,2,1792]{2,1,0:T(2,128)S(1)} %all_to_all.26.zrecv, f32[8,384]{1,0:T(8,128)S(1)} %get-tuple-element.27.moved, f32[8,384]{1,0:T(8,128)S(1)} %get-tuple-element.28.other), custom_call_target="tpu_custom_call" | custom-call | tf_op jit(solution)/shard_map/pallas_call | solution.py:331
  83.6 2.8 %all-to-all-done.3.zrecv = f32[16,1,128]{2,1,0:T(1,128)S(1)} async-done(((f32[16,1,128]{2,1,0:T(1,128)}), f32[16,1,128]{2,1,0:T(1,128)S(1)}, u32[]{:S(2)}, u32[]{:S(2)}) %all-to-all-start.3) | async-done | bytes 8224 | tf_op jit(solution)/shard_map/all_to_all | solution.py:350
  86.4 0.0 copy-start.2
  86.4 1.1 %shard_map.123 = f32[32,8,128]{2,1,0:T(8,128)S(1)} custom-call(f32[16,1,128]{2,1,0:T(1,128)S(1)} %all-to-all-done.3.zrecv, f32[8,384]{1,0:T(8,128)S(1)} %get-tuple-element.27.moved, f32[8,384]{1,0:T(8,128)S(1)} %get-tuple-element.28.other, f32[8,768]{1,0:T(8,128)S(1)} %shard_map.122.part), custom_call_target="tpu_custom_call" | custom-call | tf_op jit(solution)/shard_map/pallas_call | solution.py:331
  87.5 0.0 copy-start
  87.5 0.0 copy-start.1
  87.6 12.8 %all_to_all.28.frecv = f32[32,8,128]{2,1,0:T(8,128)S(1)} all-to-all(f32[32,8,128]{2,1,0:T(8,128)S(1)} %shard_map.123), channel_id=1, replica_groups=mesh['a'=2,'b'=2,'h'=2,'z'=16,'l'=2,'c'=2] {'a','b','h','l','c'}, dimensions={0} | all-to-all | bytes 262144 | tf_op jit(solution)/shard_map/all_to_all | solution.py:350
  100.3 0.0 copy-done.2
  100.4 0.0 copy-done
  100.4 0.0 copy-done.1
  100.4 1.1 %shard_map.124 = (f32[3,256]{1,0:T(4,128)}, f32[3,256]{1,0:T(4,128)}, f32[3,256]{1,0:T(4,128)}, f32[3,256]{1,0:T(4,128)}, f32[6,2,24]{2,1,0:T(2,128)}) custom-call(f32[16,256]{1,0:T(8,128)S(1)} %copy-done.2, f32[32,8,128]{2,1,0:T(8,128)S(1)} %all_to_all.28.frecv, f32[8,128]{1,0:T(8,128)S(1)} %get-tuple-element.29.mine, f32[256,128]{1,0:T(8,128)S(1)} %copy-done, ...), custom_call_target="tpu_custom_call" | custom-call | tf_op jit(solution)/shard_map/pallas_call | solution.py:331
Async XLA Ops:
  2.9 18.3 %copy-start.3 = (f32[16,2,1792]{2,1,0:T(2,128)S(1)}, f32[16,2,1792]{2,1,0:T(2,128)}, u32[]{:S(2)}) copy-start(f32[16,2,1792]{2,1,0:T(2,128)} %get-tuple-element.22) | copy-start | bytes 688132
  69.6 16.8 %all-to-all-start.3 = ((f32[16,1,128]{2,1,0:T(1,128)}), f32[16,1,128]{2,1,0:T(1,128)S(1)}, u32[]{:S(2)}, u32[]{:S(2)}) async-start(f32[16,1,128]{2,1,0:T(1,128)} %get-tuple-element.26), calls=%async_computation.3 | async-start | bytes 16384 | tf_op jit(solution)/shard_map/all_to_all | solution.py:350
  86.4 13.9 %copy-start.2 = (f32[16,256]{1,0:T(8,128)S(1)}, f32[16,256]{1,0:T(8,128)}, u32[]{:S(2)}) copy-start(f32[16,256]{1,0:T(8,128)} %get-tuple-element.21.keep) | copy-start | bytes 49156
  87.5 12.8 %copy-start = (f32[256,128]{1,0:T(8,128)S(1)}, f32[256,128]{1,0:T(8,128)}, u32[]{:S(2)}) copy-start(f32[256,128]{1,0:T(8,128)} %get-tuple-element.30.place) | copy-start | bytes 393220
  87.5 12.8 %copy-start.1 = (f32[2,128,24]{2,1,0:T(8,128)S(1)}, f32[2,128,24]{2,1,0:T(8,128)}, u32[]{:S(2)}) copy-start(f32[2,128,24]{2,1,0:T(8,128)} %get-tuple-element.31.slots) | copy-start | bytes 73732

commit v6 on v4

--- a/solution.py
+++ b/solution.py
@@ -19,7 +19,7 @@
 RATES = 64
 ALL_AXES = ("a", "b", "h", "z", "l", "c")
 PLANE_AXES = ("a", "b", "h", "l", "c")
-STAGES = (("l", "c"), "h", "b", "a")
+STAGES = ("l", "h", "b", "a", "c")
 EXACT = lax.Precision.HIGHEST
 F32 = jnp.float32
 I32 = jnp.int32
@@ -216,7 +216,7 @@
 
 def first_kernel(zrecv, irecv, psend, known, other, feats, values):
     for q in range(CHIPS):
-        block = irecv[2 * q] + irecv[2 * q + 1]
+        block = irecv[q] + irecv[CHIPS + q]
         here = slice(SLOTS * q, SLOTS * (q + 1))
         known[0:8, here] = block[:, 0:SLOTS]
         known[8:16, here] = block[:, RATES : RATES + SLOTS]

time: 102 us -> 102 us (level)
    all_gather x4 -> x5, blocking collectives: 20 us -> 23.2 us  [gathered(): value = lax.all_gather(value, axes, tiled=True)]
    all_to_all x2, blocking collectives: 31.8 us -> 29.1 us  [exchange(): return lax.all_to_all(value, axes, 0, 0, tiled=True)]
where the time goes in v6:
time: 102 us
  blocking collectives  52.3 us (51%)
  starting transfers between devices  27.5 us (27%)
  Pallas kernels  18.2 us (18%)
  waiting for transfers between devices  2.87 us (3%)
    all_to_all x2, blocking collectives, exchange(): return lax.all_to_all(value, axes, 0, 0, tiled=True)  29.1 us
    all_to_all x2, starting transfers between devices, exchange(): return lax.all_to_all(value, axes, 0, 0, tiled=True)  27.5 us
    all_gather x5, blocking collectives, gathered(): value = lax.all_gather(value, axes, tiled=True)  23.2 us
    pallas_call x6, Pallas kernels, call(): pl.pallas_call(kernel, out_shape=[jax.ShapeDtypeStruct(s, F32) for s in o...  18.2 us
    all_to_all x2, waiting for transfers between devices, exchange(): return lax.all_to_all(value, axes, 0, 0, tiled=True)  2.87 us
  transfers between devices with their start and end apart: 2, of which 1 were waited for; matrix products, arithmetic and copies ran while one was open for 0% of the time, Pallas kernels for 8%

profile of v6, /device:TPU:1, one launch (start us, length us, event | category | flops | bytes accessed | tf_op | source)
XLA Modules:
  0.0 101.6 jit_solution(7695668207688775691)
XLA Ops:
  0.6 2.2 %shard_map.119 = (f32[16,16,256]{2,1,0:T(8,128)}, f32[8,128]{1,0:T(8,128)}, f32[256,128]{1,0:T(8,128)}, f32[2,128,24]{2,1,0:T(8,128)}, f32[16,256]{1,0:T(8,128)}) custom-call(f32[3,256]{1,0:T(4,128)} %refs_0_.1, f32[3,256]{1,0:T(4,128)} %refs_1_.1, f32[3,256]{1,0:T(4,128)} %refs_2_.1, f32[3,256]{1,0:T(4,128)} %refs_3_.1, f32[1,256]{1,0:T(1,128)} %bitcast.6, ...), custom_call_target="tpu_custom_call" | custom-call | tf_op jit(solution)/shard_map/pallas_call | solution.py:325
  2.9 0.0 copy-start.3
  2.9 15.8 %all-to-all-start = ((f32[16,16,256]{2,1,0:T(8,128)}), f32[16,16,256]{2,1,0:T(8,128)S(1)}, u32[]{:S(2)}, u32[]{:S(2)}) async-start(f32[16,16,256]{2,1,0:T(8,128)} %get-tuple-element.22), calls=%async_computation | async-start | bytes 524288 | tf_op jit(solution)/shard_map/all_to_all | solution.py:346
  18.6 0.0 copy-done.3
  18.7 3.2 %all_gather.15 = f32[16,128]{1,0:T(8,128)S(1)} all-gather(f32[8,128]{1,0:T(8,128)S(1)} %copy-done.3), channel_id=1, replica_groups=mesh['a'=2,'b'=2,'h'=2,'z'=16,'l'=2,'c'=2] {'l'}, dimensions={0}, use_global_device_ids=true | all-gather | bytes 12288 | tf_op jit(solution)/shard_map/all_gather | solution.py:341
  21.8 5.0 %all_gather.16 = f32[32,128]{1,0:T(8,128)S(1)} all-gather(f32[16,128]{1,0:T(8,128)S(1)} %all_gather.15), channel_id=1, replica_groups=mesh['a'=2,'b'=2,'h'=2,'z'=16,'l'=2,'c'=2] {'h'}, dimensions={0}, use_global_device_ids=true | all-gather | bytes 24576 | tf_op jit(solution)/shard_map/all_gather | solution.py:341
  26.8 3.5 %all_gather.17 = f32[64,128]{1,0:T(8,128)S(1)} all-gather(f32[32,128]{1,0:T(8,128)S(1)} %all_gather.16), channel_id=1, replica_groups=mesh['a'=2,'b'=2,'h'=2,'z'=16,'l'=2,'c'=2] {'b'}, dimensions={0}, use_global_device_ids=true | all-gather | bytes 49152 | tf_op jit(solution)/shard_map/all_gather | solution.py:341
  30.4 5.2 %all_gather.18 = f32[128,128]{1,0:T(8,128)S(1)} all-gather(f32[64,128]{1,0:T(8,128)S(1)} %all_gather.17), channel_id=1, replica_groups=mesh['a'=2,'b'=2,'h'=2,'z'=16,'l'=2,'c'=2] {'a'}, dimensions={0}, use_global_device_ids=true | all-gather | bytes 98304 | tf_op jit(solution)/shard_map/all_gather | solution.py:341
  35.6 6.2 %all_gather.19 = f32[256,128]{1,0:T(8,128)S(1)} all-gather(f32[128,128]{1,0:T(8,128)S(1)} %all_gather.18), channel_id=1, replica_groups=mesh['a'=2,'b'=2,'h'=2,'z'=16,'l'=2,'c'=2] {'c'}, dimensions={0}, use_global_device_ids=true | all-gather | bytes 196608 | tf_op jit(solution)/shard_map/all_gather | solution.py:341
  41.8 0.0 all-to-all-done.zrecv
  41.8 4.4 %shard_map.120 = (f32[32,2,1152]{2,1,0:T(2,128)S(1)}, f32[16,384]{1,0:T(8,128)S(1)}, f32[8,384]{1,0:T(8,128)S(1)}) custom-call(f32[16,16,256]{2,1,0:T(8,128)S(1)} %all-to-all-done.zrecv, f32[32,8,128]{2,1,0:T(8,128)S(1)} %bitcast.5), custom_call_target="tpu_custom_call" | custom-call | tf_op jit(solution)/shard_map/pallas_call | solution.py:325
  46.3 16.5 %all_to_all.20.precv = f32[32,2,1152]{2,1,0:T(2,128)S(1)} all-to-all(f32[32,2,1152]{2,1,0:T(2,128)S(1)} %get-tuple-element.24), channel_id=1, replica_groups=mesh['a'=2,'b'=2,'h'=2,'z'=16,'l'=2,'c'=2] {'a','b','h','l','c'}, dimensions={0} | all-to-all | bytes 589824 | tf_op jit(solution)/shard_map/all_to_all | solution.py:346
  62.8 0.9 shard_map.121
  63.7 11.7 %all-to-all-start.2 = ((f32[16,1,128]{2,1,0:T(1,128)}), f32[16,1,128]{2,1,0:T(1,128)S(1)}, u32[]{:S(2)}, u32[]{:S(2)}) async-start(f32[16,1,128]{2,1,0:T(1,128)} %get-tuple-element.26), calls=%async_computation.2 | async-start | bytes 16384 | tf_op jit(solution)/shard_map/all_to_all | solution.py:346
  75.4 8.4 %shard_map.122.part = f32[8,768]{1,0:T(8,128)S(1)} custom-call(f32[16,16,256]{2,1,0:T(8,128)S(1)} %all-to-all-done.zrecv, f32[8,384]{1,0:T(8,128)S(1)} %get-tuple-element.27.moved, f32[8,384]{1,0:T(8,128)S(1)} %get-tuple-element.28.other), custom_call_target="tpu_custom_call" | custom-call | tf_op jit(solution)/shard_map/pallas_call | solution.py:325
  83.8 2.9 %all-to-all-done.2.zrecv = f32[16,1,128]{2,1,0:T(1,128)S(1)} async-done(((f32[16,1,128]{2,1,0:T(1,128)}), f32[16,1,128]{2,1,0:T(1,128)S(1)}, u32[]{:S(2)}, u32[]{:S(2)}) %all-to-all-start.2) | async-done | bytes 8224 | tf_op jit(solution)/shard_map/all_to_all | solution.py:346
  86.7 0.0 copy-start.2
  86.7 1.1 %shard_map.123 = f32[32,8,128]{2,1,0:T(8,128)S(1)} custom-call(f32[16,1,128]{2,1,0:T(1,128)S(1)} %all-to-all-done.2.zrecv, f32[8,384]{1,0:T(8,128)S(1)} %get-tuple-element.27.moved, f32[8,384]{1,0:T(8,128)S(1)} %get-tuple-element.28.other, f32[8,768]{1,0:T(8,128)S(1)} %shard_map.122.part), custom_call_target="tpu_custom_call" | custom-call | tf_op jit(solution)/shard_map/pallas_call | solution.py:325
  87.8 0.0 copy-start
  87.8 0.0 copy-start.1
  87.9 12.7 %all_to_all.21.frecv = f32[32,8,128]{2,1,0:T(8,128)S(1)} all-to-all(f32[32,8,128]{2,1,0:T(8,128)S(1)} %shard_map.123), channel_id=1, replica_groups=mesh['a'=2,'b'=2,'h'=2,'z'=16,'l'=2,'c'=2] {'a','b','h','l','c'}, dimensions={0} | all-to-all | bytes 262144 | tf_op jit(solution)/shard_map/all_to_all | solution.py:346
  100.5 0.0 copy-done.2
  100.5 0.0 copy-done
  100.5 0.0 copy-done.1
  100.5 1.1 %shard_map.124 = (f32[3,256]{1,0:T(4,128)}, f32[3,256]{1,0:T(4,128)}, f32[3,256]{1,0:T(4,128)}, f32[3,256]{1,0:T(4,128)}, f32[6,2,24]{2,1,0:T(2,128)}) custom-call(f32[16,256]{1,0:T(8,128)S(1)} %copy-done.2, f32[32,8,128]{2,1,0:T(8,128)S(1)} %all_to_all.21.frecv, f32[8,128]{1,0:T(8,128)S(1)} %get-tuple-element.29.mine, f32[256,128]{1,0:T(8,128)S(1)} %copy-done, ...), custom_call_target="tpu_custom_call" | custom-call | tf_op jit(solution)/shard_map/pallas_call | solution.py:325
Async XLA Ops:
  2.9 15.8 %copy-start.3 = (f32[8,128]{1,0:T(8,128)S(1)}, f32[8,128]{1,0:T(8,128)}, u32[]{:S(2)}) copy-start(f32[8,128]{1,0:T(8,128)} %get-tuple-element.23) | copy-start | bytes 12292
  2.9 39.0 %all-to-all-start = ((f32[16,16,256]{2,1,0:T(8,128)}), f32[16,16,256]{2,1,0:T(8,128)S(1)}, u32[]{:S(2)}, u32[]{:S(2)}) async-start(f32[16,16,256]{2,1,0:T(8,128)} %get-tuple-element.22), calls=%async_computation | async-start | bytes 524288 | tf_op jit(solution)/shard_map/all_to_all | solution.py:346
  63.7 23.0 %all-to-all-start.2 = ((f32[16,1,128]{2,1,0:T(1,128)}), f32[16,1,128]{2,1,0:T(1,128)S(1)}, u32[]{:S(2)}, u32[]{:S(2)}) async-start(f32[16,1,128]{2,1,0:T(1,128)} %get-tuple-element.26), calls=%async_computation.2 | async-start | bytes 16384 | tf_op jit(solution)/shard_map/all_to_all | solution.py:346
  86.7 13.8 %copy-start.2 = (f32[16,256]{1,0:T(8,128)S(1)}, f32[16,256]{1,0:T(8,128)}, u32[]{:S(2)}) copy-start(f32[16,256]{1,0:T(8,128)} %get-tuple-element.21.keep) | copy-start | bytes 49156
  87.8 12.7 %copy-start = (f32[256,128]{1,0:T(8,128)S(1)}, f32[256,128]{1,0:T(8,128)}, u32[]{:S(2)}) copy-start(f32[256,128]{1,0:T(8,128)} %get-tuple-element.30.place) | copy-start | bytes 393220
  87.8 12.7 %copy-start.1 = (f32[2,128,24]{2,1,0:T(8,128)S(1)}, f32[2,128,24]{2,1,0:T(8,128)}, u32[]{:S(2)}) copy-start(f32[2,128,24]{2,1,0:T(8,128)} %get-tuple-element.31.slots) | copy-start | bytes 73732
